TPU v7x, 256 devices: a whole 4x4x8 slice. The times are simulated.
256 devices in a mesh: dp: 32 (over x, y, core), owner: 8 (over z).
Axes of the slice: x: 4, y: 4, z: 8, core: 2. Of those that a mesh axis runs over, the one named last changes fastest.
Arguments:
- momentum: float32 [192, 1024, 768], P(None, ('dp', 'owner')), may hold values from -6 to 6
- grad: bfloat16 [192, 1024, 768], P(None, ('dp', 'owner'))
- owner_table: int32 [192], replicated, may hold values from 0 to 255, as said below
Outputs:
- new_momentum: float32 [192, 1024, 768], P(None, ('dp', 'owner'))
- update: float32 [192, 1024, 768], P(None, ('dp', 'owner'))
- owned_update: bfloat16 [2, 256, 1024, 768], P(None, ('dp', 'owner'))
Inputs may be any that keep to these rules, and one draw needn't show every extreme that they name: `owner_table`: no device owns more than 2 matrices, and some device owns exactly 2.
All inputs are finite; a program needn't handle non-finite values.
Results may differ from a plain program's by a relative error of at most 0.0073.
Values may be sent and summed in bfloat16 or wider, within the bound.
No kernel may reach another device: no remote copies, remote signals or barrier semaphores. Data moves between devices by JAX's collectives and lax.ppermute only.
A program may use at most 64 MiB of HBM per device.

v0:
```python
import functools
import math

import jax
import jax.numpy as jnp
from jax import lax
from jax.experimental import pallas as pl
from jax.experimental.pallas import tpu as pltpu
from jax.sharding import PartitionSpec as P

ITERS = 2
CAP = 2

momentum_decay = 0.95
quintic_one = 3.4445
quintic_two = -4.775
quintic_three = 2.0315
norm_epsilon = 1e-07

SLOT, FIRST, SECOND, SPILLED, PART, INDEX, EARLY, HELPER_INDEX, HELPER_EARLY = range(9)
TABLE_ROWS = 16


def table_kernel(planes, place_ref, owner_ref, table_ref):
    mats = owner_ref.shape[1]
    devices = table_ref.shape[1]
    f32 = jnp.float32

    def iota(rows, cols, axis):
        return lax.broadcasted_iota(jnp.int32, (rows, cols), axis)

    def total(cond, axis):
        return jnp.sum(jnp.where(cond, 1.0, 0.0).astype(f32), axis=axis, keepdims=True)

    def column(row):
        n = row.shape[1]
        return jnp.sum(jnp.where(iota(n, n, 0) == iota(n, n, 1), row, 0.0), axis=1, keepdims=True)

    own_row = owner_ref[...].astype(f32)
    own_col = column(own_row)
    same = own_col == own_row
    rank_row = total(same & (iota(mats, mats, 0) < iota(mats, mats, 1)), 0)
    rank_col = total(same & (iota(mats, mats, 1) < iota(mats, mats, 0)), 1)
    held = own_col == iota(mats, devices, 1).astype(f32)
    first_row = total(held & (rank_col == 0.0), 0)
    second_row = total(held & (rank_col == 1.0), 0)
    held = own_row == iota(devices, mats, 0).astype(f32)
    first_col = total(held & (rank_row == 0.0), 1)
    second_col = total(held & (rank_row == 1.0), 1)
    up, down = iota(devices, devices, 0), iota(devices, devices, 1)
    plane = (up & (planes - 1)) == (down & (planes - 1))
    before_row, before_col = up < down, down < up
    free_index = total(before_col & plane & (first_row == 0.0), 1)
    second_index = total(before_row & plane & (second_col == 1.0), 0)
    pair = plane & (first_col == 0.0) & (second_row == 1.0) & (free_index == second_index)
    left_row = second_row - total(pair, 0)
    idle_col = 1.0 - first_col - total(pair, 1)
    left_col = column(left_row)
    idle_row = jnp.sum(jnp.where(up == down, idle_col, 0.0), axis=0, keepdims=True)
    left_index = total(before_row & (left_col == 1.0), 0)
    idle_index = total(before_col & (idle_row == 1.0), 1)
    spill = (left_row == 1.0) & (idle_col == 1.0) & (left_index == idle_index)
    helper_row = jnp.sum(jnp.where(pair | spill, up.astype(f32), 0.0), axis=0, keepdims=True)
    helper_col = column(helper_row)
    helper_of = jnp.sum(jnp.where(held, helper_col, 0.0), axis=0, keepdims=True)
    slot_row = jnp.where(rank_row == 0.0, own_row, helper_of)
    spilled = jnp.sum(left_row, axis=1, keepdims=True)
    slot_row = slot_row.astype(jnp.int32)
    helper_row = helper_row.astype(jnp.int32)
    shift = planes.bit_length() - 1
    count = devices // planes

    def late_index(slot):
        return ((place_ref[0] - slot) & (planes - 1)) * count + (slot >> shift)

    def early_index(slot):
        return (slot >> shift) * planes + ((place_ref[0] - slot) & (planes - 1))

    mine = up == (down * planes + place_ref[0])
    helper_here = column(helper_row.astype(f32))
    part_row = jnp.sum(jnp.where(mine, helper_here, 0.0), axis=0, keepdims=True).astype(jnp.int32) >> shift

    def put(row, values):
        table_ref[row : row + 1, : values.shape[1]] = values.astype(jnp.int32)

    table_ref[...] = jnp.zeros_like(table_ref)
    put(SLOT, slot_row)
    put(FIRST, first_row)
    put(SECOND, second_row)
    put(SPILLED, jnp.broadcast_to(spilled, (1, devices)))
    put(PART, part_row)
    put(INDEX, late_index(slot_row))
    put(EARLY, early_index(slot_row))
    put(HELPER_INDEX, late_index(helper_row))
    put(HELPER_EARLY, early_index(helper_row))


def make_table(owner_table, place, planes, devices):
    mats = owner_table.shape[0]
    return pl.pallas_call(
        functools.partial(table_kernel, planes),
        grid_spec=pltpu.PrefetchScalarGridSpec(
            num_scalar_prefetch=1,
            grid=(1,),
            in_specs=[pl.BlockSpec((1, mats), lambda *_: (0, 0))],
            out_specs=pl.BlockSpec((TABLE_ROWS, devices), lambda *_: (0, 0)),
        ),
        out_shape=jax.ShapeDtypeStruct((TABLE_ROWS, devices), jnp.int32),
        name="table",
    )(place, owner_table.reshape(1, mats))


def momentum_kernel(table_ref, momentum_ref, grad_ref, new_ref, out_ref):
    step = pl.program_id(0)
    block = momentum_ref.shape[0]

    @pl.when(step == 0)
    def _():
        out_ref[...] = jnp.zeros_like(out_ref)

    for i in range(block):
        grad = grad_ref[i].astype(jnp.float32)
        new = momentum_decay * momentum_ref[i] + grad
        new_ref[i] = new
        slot = table_ref[SLOT, step * block + i]
        out_ref[slot] = (grad + momentum_decay * new).astype(out_ref.dtype)


def momentum_step(table, momentum, grad, devices, block=24):
    mats, rows, cols = momentum.shape
    while mats % block:
        block -= 1

    def block_spec():
        return pl.BlockSpec((block, rows, cols), lambda i, *_: (i, 0, 0))

    return pl.pallas_call(
        momentum_kernel,
        grid_spec=pltpu.PrefetchScalarGridSpec(
            num_scalar_prefetch=1,
            grid=(mats // block,),
            in_specs=[block_spec(), block_spec()],
            out_specs=[block_spec(), pl.BlockSpec((devices, rows, cols), lambda i, *_: (0, 0, 0))],
        ),
        out_shape=[
            jax.ShapeDtypeStruct(momentum.shape, jnp.float32),
            jax.ShapeDtypeStruct((devices, rows, cols), jnp.bfloat16),
        ],
        compiler_params=pltpu.CompilerParams(vmem_limit_bytes=60 * 1024 * 1024),
        name="momentum",
    )(table, momentum, grad)


def orthogonalize_kernel(scale, x_ref, out_ref, iterate_ref, gram_ref, poly_ref):
    rows, cols = x_ref.shape
    tile = min(256, rows)
    f32, bf16 = jnp.float32, jnp.bfloat16

    def poly(gram):
        gram_ref[...] = gram.astype(bf16)
        square = jnp.dot(gram_ref[...], gram_ref[...], preferred_element_type=f32)
        poly_ref[...] = (quintic_two * gram_ref[...].astype(f32) + quintic_three * square).astype(bf16)

    def apply(source_ref, target_ref, factor, last):
        for i in range(rows // tile):
            part = source_ref[i * tile : (i + 1) * tile, :]
            step = quintic_one * part.astype(f32) + jnp.dot(part, poly_ref[...], preferred_element_type=f32)
            step = (step * factor).astype(bf16) if factor is not None else step.astype(bf16)
            target_ref[i * tile : (i + 1) * tile, :] = step * jnp.asarray(scale, bf16) if last else step

    def gram_of(ref):
        return lax.dot_general(ref[...], ref[...], (((0,), (0,)), ((), ())), preferred_element_type=f32)

    gram = gram_of(x_ref)
    diagonal = lax.broadcasted_iota(jnp.int32, (cols, cols), 0) == lax.broadcasted_iota(jnp.int32, (cols, cols), 1)
    trace = jnp.sum(jnp.sum(jnp.where(diagonal, gram, 0.0), axis=0, keepdims=True), axis=1, keepdims=True)
    factor = 1.0 / (jnp.sqrt(trace) + norm_epsilon)
    poly(gram * factor * factor)
    apply(x_ref, iterate_ref, factor, False)
    for step in range(1, ITERS):
        poly(gram_of(iterate_ref))
        apply(iterate_ref, out_ref, None, True)


def orthogonalize(matrix, scale):
    rows, cols = matrix.shape
    return pl.pallas_call(
        functools.partial(orthogonalize_kernel, scale),
        out_shape=jax.ShapeDtypeStruct((rows, cols), jnp.bfloat16),
        scratch_shapes=[
            pltpu.VMEM((rows, cols), jnp.bfloat16),
            pltpu.VMEM((cols, cols), jnp.bfloat16),
            pltpu.VMEM((cols, cols), jnp.bfloat16),
        ],
        compiler_params=pltpu.CompilerParams(vmem_limit_bytes=40 * 1024 * 1024),
        cost_estimate=pl.CostEstimate(flops=ITERS * 2 * cols * cols * (2 * rows + cols), bytes_accessed=4 * rows * cols, transcendentals=0),
        name="orthogonalize",
    )(matrix)


def pack_kernel(table_ref, place_ref, parts_ref, early_ref, out_ref):
    count, _, cols = parts_ref.shape
    out_ref[:, :, cols:] = early_ref[...]

    def each(i, _):
        out_ref[i, :, :cols] = parts_ref[table_ref[PART, i]]

    lax.fori_loop(0, count, each, None, unroll=True)


def pack(table, place, parts, early):
    count, rows, cols = parts.shape
    shape = (count, rows, cols + early.shape[2])
    return pl.pallas_call(
        pack_kernel,
        grid_spec=pltpu.PrefetchScalarGridSpec(
            num_scalar_prefetch=2,
            grid=(1,),
            in_specs=[pl.BlockSpec(x.shape, lambda *_: (0, 0, 0)) for x in (parts, early)],
            out_specs=pl.BlockSpec(shape, lambda *_: (0, 0, 0)),
        ),
        out_shape=jax.ShapeDtypeStruct(shape, parts.dtype),
        compiler_params=pltpu.CompilerParams(vmem_limit_bytes=24 * 1024 * 1024),
        name="pack",
    )(table, place, parts, early)


def finish_kernel(table_ref, place_ref, late_ref, early_ref, mine_ref, second_ref, update_ref, owned_ref):
    step = pl.program_id(0)
    block = update_ref.shape[0]
    late_cols = late_ref.shape[2]
    for i in range(block):
        index = table_ref[INDEX, step * block + i]
        update_ref[i, :, :late_cols] = late_ref[index].astype(jnp.float32)
        index = table_ref[EARLY, step * block + i]
        update_ref[i, :, late_cols:] = early_ref[index].astype(jnp.float32)
    me = place_ref[1]
    write_owned(table_ref, me, mine_ref[...], second_ref, owned_ref)


def write_owned(table_ref, me, mine, second_ref, owned_ref):
    cols = mine.shape[1]
    second = second_ref[...].reshape(mine.shape[0], second_ref.shape[2])[:, :cols]
    owned_ref[0] = jnp.where(table_ref[FIRST, me] > 0, mine, jnp.zeros_like(mine))
    owned_ref[1] = jnp.where(table_ref[SECOND, me] > 0, second, jnp.zeros_like(second))


def finish(table, place, late, early, mine, second, mats, steps=8):
    while mats % steps or second.shape[0] % steps:
        steps -= 1
    _, rows, _ = late.shape
    whole_rows, cols = mine.shape
    second_block = (second.shape[0] // steps, *second.shape[1:])
    return pl.pallas_call(
        finish_kernel,
        grid_spec=pltpu.PrefetchScalarGridSpec(
            num_scalar_prefetch=2,
            grid=(steps,),
            in_specs=[
                pl.BlockSpec(late.shape, lambda i, *_: (0, 0, 0)),
                pl.BlockSpec(early.shape, lambda i, *_: (0, 0, 0)),
                pl.BlockSpec((whole_rows // steps, cols), lambda i, *_: (i, 0)),
                pl.BlockSpec(second_block, lambda i, *_: (i, 0, 0)),
            ],
            out_specs=[
                pl.BlockSpec((mats // steps, rows, cols), lambda i, *_: (i, 0, 0)),
                pl.BlockSpec((CAP, whole_rows // steps, cols), lambda i, *_: (0, i, 0)),
            ],
        ),
        out_shape=[
            jax.ShapeDtypeStruct((mats, rows, cols), jnp.float32),
            jax.ShapeDtypeStruct((CAP, whole_rows, cols), mine.dtype),
        ],
        compiler_params=pltpu.CompilerParams(vmem_limit_bytes=32 * 1024 * 1024),
        name="finish",
    )(table, place, late, early, mine, second)


def spilled_kernel(table_ref, place_ref, late_ref, early_ref, out_ref):
    late_cols = late_ref.shape[2]

    def each(i, _):
        out_ref[i, :, :late_cols] = late_ref[table_ref[HELPER_INDEX, i]]
        out_ref[i, :, late_cols:] = early_ref[table_ref[HELPER_EARLY, i]]

    lax.fori_loop(0, out_ref.shape[0], each, None)


def spilled_rows(table, place, late, early):
    shape = (late.shape[0], late.shape[1], late.shape[2] + early.shape[2])
    return pl.pallas_call(
        spilled_kernel,
        grid_spec=pltpu.PrefetchScalarGridSpec(
            num_scalar_prefetch=2,
            grid=(1,),
            in_specs=[pl.BlockSpec(x.shape, lambda *_: (0, 0, 0)) for x in (late, early)],
            out_specs=pl.BlockSpec(shape, lambda *_: (0, 0, 0)),
        ),
        out_shape=jax.ShapeDtypeStruct(shape, late.dtype),
        compiler_params=pltpu.CompilerParams(vmem_limit_bytes=32 * 1024 * 1024),
        name="spilled",
    )(table, place, late, early)


def replace_kernel(table_ref, place_ref, mine_ref, second_ref, owned_ref):
    write_owned(table_ref, place_ref[1], mine_ref[...], second_ref, owned_ref)


def replace_owned(table, place, mine, second):
    shape = (CAP, *mine.shape)
    return pl.pallas_call(
        replace_kernel,
        grid_spec=pltpu.PrefetchScalarGridSpec(
            num_scalar_prefetch=2,
            grid=(1,),
            in_specs=[
                pl.BlockSpec(mine.shape, lambda *_: (0, 0)),
                pl.BlockSpec(second.shape, lambda *_: (0, 0, 0)),
            ],
            out_specs=pl.BlockSpec(shape, lambda *_: (0, 0, 0)),
        ),
        out_shape=jax.ShapeDtypeStruct(shape, mine.dtype),
        compiler_params=pltpu.CompilerParams(vmem_limit_bytes=32 * 1024 * 1024),
        name="replace",
    )(table, place, mine, second)


def send_planes(rows, axis):
    planes = lax.axis_size("owner")
    me = lax.axis_index("owner")

    def to_plane(far):
        return lax.dynamic_index_in_dim(rows, lax.rem(me + far, planes), axis, keepdims=False)

    arrived = {0: to_plane(0)}
    for far in sorted(range(1, planes), key=lambda far: -min(far, planes - far)):
        arrived[far] = lax.ppermute(to_plane(far), "owner", [(i, (i + far) % planes) for i in range(planes)])
    return [arrived[far] for far in range(planes)]


def shards(momentum, grad, owner_table):
    dp_count = lax.axis_size("dp")
    planes = lax.axis_size("owner")
    devices = dp_count * planes
    mats, rows, cols = momentum.shape
    whole_rows = devices * rows
    late_cols = cols - cols // 3 if cols % 384 == 0 else cols - 128
    my_plane = lax.axis_index("owner")
    place = jnp.stack([my_plane, lax.axis_index("dp") * planes + my_plane]).astype(jnp.int32)
    with jax.named_scope("table"):
        table = make_table(owner_table, place, planes, devices)
    with jax.named_scope("momentum"):
        new_momentum, outgoing = momentum_step(table, momentum, grad, devices)
    with jax.named_scope("gather_matrix"):
        received = lax.all_to_all(outgoing, ("dp", "owner"), 0, 0, tiled=True)
        matrix = received.reshape(whole_rows, cols)
    with jax.named_scope("orthogonalize"):
        mine = orthogonalize(matrix, math.sqrt(whole_rows))
    with jax.named_scope("return_dp"):
        parts = lax.all_to_all(mine.reshape(dp_count, planes * rows, cols), "dp", 0, 0, tiled=True)
    with jax.named_scope("return_owner_early"):
        early = send_planes(mine.reshape(dp_count, planes, rows, cols)[..., late_cols:], 1)
        early = jnp.stack(early, 1).reshape(dp_count, planes * rows, cols - late_cols)
    with jax.named_scope("return_owner"):
        late = jnp.concatenate(send_planes(parts.reshape(dp_count, planes, rows, cols)[..., :late_cols], 1))
    with jax.named_scope("second_matrix"):
        second = lax.all_to_all(pack(table, place, parts, early), "dp", 0, 0, tiled=True)
        early = second[..., cols:].reshape(devices, rows, cols - late_cols)
    with jax.named_scope("finish"):
        update, owned = finish(table, place, late, early, mine, second, mats)

    def with_spilled(owned, late, early):
        rows_out = lax.all_to_all(spilled_rows(table, place, late, early), ("dp", "owner"), 0, 0, tiled=True)
        return replace_owned(table, place, mine, rows_out.reshape(dp_count, planes * rows, cols))

    with jax.named_scope("spilled"):
        spilled = table[SPILLED, 0] > 0
        owned = lax.cond(spilled, with_spilled, lambda owned, late, early: owned, owned, late, early)
    return new_momentum, update, owned[:, None]


def solution(mesh):
    in_specs = (P(None, ("dp", "owner"), None), P(None, ("dp", "owner"), None), P())
    out_specs = (
        P(None, ("dp", "owner"), None),
        P(None, ("dp", "owner"), None),
        P(None, ("dp", "owner"), None, None),
    )
    return jax.shard_map(shards, mesh=mesh, in_specs=in_specs, out_specs=out_specs, check_vma=False)
```

profile of v0, /device:TPU:34, one launch (start us, length us, event | category | flops | bytes accessed | tf_op | source)
XLA Modules:
  0.0 162.4 jit_solution(648677698222064174)
XLA Ops:
  0.6 0.1 pad_add_fusion.place_ref
  0.7 2.0 %table.1.table_ref = s32[16,256]{1,0:T(8,128)S(1)} custom-call(s32[2]{0:T(128)S(1)} %pad_add_fusion.place_ref, s32[1,192]{1,0:T(1,128)} %bitcast.68), custom_call_target="tpu_custom_call" | custom-call | tf_op jit(solution)/shard_map/table/table/pallas_call | solution.py:100
  2.8 7.6 %momentum.1 = (f32[192,4,768]{2,1,0:T(4,128)}, bf16[256,4,768]{2,1,0:T(4,128)(2,1)}) custom-call(s32[16,256]{1,0:T(8,128)S(1)} %table.1.table_ref, f32[192,4,768]{2,1,0:T(4,128)} %momentum_ref.1, bf16[192,4,768]{2,1,0:T(4,128)(2,1)} %grad_ref.1), custom_call_target="tpu_custom_call" | custom-call | tf_op jit(solution)/shard_map/momentum/momentum/pallas_call | solution.py:137
  10.4 14.4 %all-to-all-start.1 = ((bf16[256,4,768]{2,1,0:T(4,128)(2,1)}), bf16[256,4,768]{2,1,0:T(4,128)(2,1)S(1)}, u32[]{:S(2)}, u32[]{:S(2)}) async-start(bf16[256,4,768]{2,1,0:T(4,128)(2,1)} %get-tuple-element.33), calls=%async_computation.1 | async-start | bytes 3145728 | tf_op jit(solution)/shard_map/gather_matrix/all_to_all | solution.py:355
  24.8 42.1 %all-to-all-done.1 = bf16[256,4,768]{2,1,0:T(4,128)(2,1)S(1)} async-done(((bf16[256,4,768]{2,1,0:T(4,128)(2,1)}), bf16[256,4,768]{2,1,0:T(4,128)(2,1)S(1)}, u32[]{:S(2)}, u32[]{:S(2)}) %all-to-all-start.1) | async-done | bytes 1572896 | tf_op jit(solution)/shard_map/gather_matrix/all_to_all | solution.py:355
  66.9 0.4 reshape.35.x_ref
  67.3 9.4 %orthogonalize.1.mine_ref = bf16[1024,768]{1,0:T(8,128)(2,1)} custom-call(bf16[1024,768]{1,0:T(8,128)(2,1)S(1)} %reshape.35.x_ref), custom_call_target="tpu_custom_call" | custom-call | flops 6643777536 | bytes 3145728 | tf_op jit(solution)/shard_map/orthogonalize/orthogonalize/pallas_call | solution.py:187
  76.7 2.9 %reshape.38 = bf16[32,8,4,768]{3,2,1,0:T(4,128)(2,1)S(1)} reshape(bf16[1024,768]{1,0:T(8,128)(2,1)} %orthogonalize.1.mine_ref) | data formatting | bytes 3145728 | tf_op jit(solution)/shard_map/return_owner_early/reshape | solution.py:362
  79.6 0.2 slice.17
  79.8 0.3 dynamic-slice_bitcast_fusion.7
  80.1 0.4 collective-permute-start.7
  80.5 5.1 %all-to-all-start.2 = ((bf16[32,32,768]{2,1,0:T(8,128)(2,1)}), bf16[32,32,768]{2,1,0:T(8,128)(2,1)S(1)}, u32[]{:S(2)}, u32[]{:S(2)}) async-start(bf16[32,32,768]{2,1,0:T(8,128)(2,1)} %bitcast.3), calls=%async_computation.2 | async-start | bytes 3145728 | tf_op jit(solution)/shard_map/return_dp/all_to_all | solution.py:360
  85.6 1.1 collective-permute-start.8
  86.7 1.3 collective-permute-start.9
  87.9 4.9 %collective-permute-start.10 = (bf16[32,4,256]{2,1,0:T(4,128)(2,1)S(1)}, bf16[32,4,256]{2,1,0:T(4,128)(2,1)S(1)}, u32[]{:S(2)}, u32[]{:S(2)}) collective-permute-start(bf16[32,4,256]{2,1,0:T(4,128)(2,1)S(1)} %get-tuple-element.51), channel_id=1, source_target_pairs={{0,4},{1,5},{2,6},{3,7},{4,0},{5,1},{6,2},{7,3},{8,12},{9,13},{10,... | collective-permute-start | bytes 196616 | tf_op jit(solution)/shard_map/return_owner_early/ppermute | solution.py:337
  92.9 3.7 %collective-permute-start.11 = (bf16[32,4,256]{2,1,0:T(4,128)(2,1)S(1)}, bf16[32,4,256]{2,1,0:T(4,128)(2,1)S(1)}, u32[]{:S(2)}, u32[]{:S(2)}) collective-permute-start(bf16[32,4,256]{2,1,0:T(4,128)(2,1)S(1)} %get-tuple-element.50), channel_id=1, source_target_pairs={{0,5},{1,6},{2,7},{3,0},{4,1},{5,2},{6,3},{7,4},{8,13},{9,14},{10,... | collective-permute-start | bytes 196616 | tf_op jit(solution)/shard_map/return_owner_early/ppermute | solution.py:337
  96.6 0.0 collective-permute-done.7
  96.6 0.0 collective-permute-start.12
  96.6 0.0 collective-permute-done.8
  96.6 3.1 %collective-permute-start.13 = (bf16[32,4,256]{2,1,0:T(4,128)(2,1)S(1)}, bf16[32,4,256]{2,1,0:T(4,128)(2,1)S(1)}, u32[]{:S(2)}, u32[]{:S(2)}) collective-permute-start(bf16[32,4,256]{2,1,0:T(4,128)(2,1)S(1)} %get-tuple-element.48), channel_id=1, source_target_pairs={{0,7},{1,0},{2,1},{3,2},{4,3},{5,4},{6,5},{7,6},{8,15},{9,8},{10,9... | collective-permute-start | bytes 196616 | tf_op jit(solution)/shard_map/return_owner_early/ppermute | solution.py:337
  99.8 1.0 collective-permute-done.9
  100.8 0.0 collective-permute-done.10
  100.8 4.0 %collective-permute-done.11 = bf16[32,4,256]{2,1,0:T(4,128)(2,1)S(1)} collective-permute-done((bf16[32,4,256]{2,1,0:T(4,128)(2,1)S(1)}, bf16[32,4,256]{2,1,0:T(4,128)(2,1)S(1)}, u32[]{:S(2)}, u32[]{:S(2)}) %collective-permute-start.11) | collective-permute-done | bytes 65568 | tf_op jit(solution)/shard_map/return_owner_early/ppermute | solution.py:337
  104.9 0.0 collective-permute-done.12
  105.0 0.3 collective-permute-done.13
  105.3 0.1 reshape.39.early_ref
  105.4 0.4 all-to-all-done.2.parts_ref
  105.8 1.0 pack.1
  106.8 0.0 copy-start
  106.8 1.3 copy-done
  108.1 7.6 %all-to-all-start.3 = ((bf16[32,32,1024]{2,1,0:T(8,128)(2,1)}), bf16[32,32,1024]{2,1,0:T(8,128)(2,1)}, u32[]{:S(2)}, u32[]{:S(2)}) async-start(bf16[32,32,1024]{2,1,0:T(8,128)(2,1)} %copy-done), calls=%async_computation.3 | async-start | bytes 4194304 | tf_op jit(solution)/shard_map/second_matrix/all_to_all | solution.py:367
  115.7 0.4 reshape.37
  116.1 0.4 slice.16
  116.6 0.5 dynamic-slice_bitcast_fusion
  117.0 1.3 collective-permute-start
  118.4 0.5 slice.19
  119.6 2.2 %collective-permute-start.1 = (bf16[32,4,512]{2,1,0:T(4,128)(2,1)S(1)}, bf16[32,4,512]{2,1,0:T(4,128)(2,1)S(1)}, u32[]{:S(2)}, u32[]{:S(2)}) collective-permute-start(bf16[32,4,512]{2,1,0:T(4,128)(2,1)S(1)} %get-tuple-element.46), channel_id=1, source_target_pairs={{0,2},{1,3},{2,4},{3,5},{4,6},{5,7},{6,0},{7,1},{8,10},{9,11},{10,... | collective-permute-start | bytes 393224 | tf_op jit(solution)/shard_map/return_owner/ppermute | solution.py:337
  121.7 0.1 bitcast_dynamic-update-slice_fusion
  121.8 2.9 %collective-permute-start.2 = (bf16[32,4,512]{2,1,0:T(4,128)(2,1)S(1)}, bf16[32,4,512]{2,1,0:T(4,128)(2,1)S(1)}, u32[]{:S(2)}, u32[]{:S(2)}) collective-permute-start(bf16[32,4,512]{2,1,0:T(4,128)(2,1)S(1)} %get-tuple-element.45), channel_id=1, source_target_pairs={{0,3},{1,4},{2,5},{3,6},{4,7},{5,0},{6,1},{7,2},{8,11},{9,12},{10,... | collective-permute-start | bytes 393224 | tf_op jit(solution)/shard_map/return_owner/ppermute | solution.py:337
  124.7 2.5 %collective-permute-start.3 = (bf16[32,4,512]{2,1,0:T(4,128)(2,1)S(1)}, bf16[32,4,512]{2,1,0:T(4,128)(2,1)S(1)}, u32[]{:S(2)}, u32[]{:S(2)}) collective-permute-start(bf16[32,4,512]{2,1,0:T(4,128)(2,1)S(1)} %get-tuple-element.44), channel_id=1, source_target_pairs={{0,4},{1,5},{2,6},{3,7},{4,0},{5,1},{6,2},{7,3},{8,12},{9,13},{10,... | collective-permute-start | bytes 393224 | tf_op jit(solution)/shard_map/return_owner/ppermute | solution.py:337
  127.2 3.1 %collective-permute-start.4 = (bf16[32,4,512]{2,1,0:T(4,128)(2,1)S(1)}, bf16[32,4,512]{2,1,0:T(4,128)(2,1)S(1)}, u32[]{:S(2)}, u32[]{:S(2)}) collective-permute-start(bf16[32,4,512]{2,1,0:T(4,128)(2,1)S(1)} %get-tuple-element.43), channel_id=1, source_target_pairs={{0,5},{1,6},{2,7},{3,0},{4,1},{5,2},{6,3},{7,4},{8,13},{9,14},{10,... | collective-permute-start | bytes 393224 | tf_op jit(solution)/shard_map/return_owner/ppermute | solution.py:337
  130.3 0.0 collective-permute-done
  130.3 1.0 collective-permute-start.5
  131.3 0.1 constant_dynamic-update-slice_fusion.6
  131.3 0.8 collective-permute-done.1
  132.1 2.1 %collective-permute-start.6 = (bf16[32,4,512]{2,1,0:T(4,128)(2,1)S(1)}, bf16[32,4,512]{2,1,0:T(4,128)(2,1)S(1)}, u32[]{:S(2)}, u32[]{:S(2)}) collective-permute-start(bf16[32,4,512]{2,1,0:T(4,128)(2,1)S(1)} %get-tuple-element.41), channel_id=1, source_target_pairs={{0,7},{1,0},{2,1},{3,2},{4,3},{5,4},{6,5},{7,6},{8,15},{9,8},{10,9... | collective-permute-start | bytes 393224 | tf_op jit(solution)/shard_map/return_owner/ppermute | solution.py:337
  134.2 0.1 constant_dynamic-update-slice_fusion.5
  134.3 8.2 %collective-permute-done.2 = bf16[32,4,512]{2,1,0:T(4,128)(2,1)S(1)} collective-permute-done((bf16[32,4,512]{2,1,0:T(4,128)(2,1)S(1)}, bf16[32,4,512]{2,1,0:T(4,128)(2,1)S(1)}, u32[]{:S(2)}, u32[]{:S(2)}) %collective-permute-start.2) | collective-permute-done | bytes 131104 | tf_op jit(solution)/shard_map/return_owner/ppermute | solution.py:337
  142.5 0.1 constant_dynamic-update-slice_fusion.4
  142.5 0.0 collective-permute-done.3
  142.5 0.1 constant_dynamic-update-slice_fusion.3
  142.6 3.4 %collective-permute-done.4 = bf16[32,4,512]{2,1,0:T(4,128)(2,1)S(1)} collective-permute-done((bf16[32,4,512]{2,1,0:T(4,128)(2,1)S(1)}, bf16[32,4,512]{2,1,0:T(4,128)(2,1)S(1)}, u32[]{:S(2)}, u32[]{:S(2)}) %collective-permute-start.4) | collective-permute-done | bytes 131104 | tf_op jit(solution)/shard_map/return_owner/ppermute | solution.py:337
  146.0 0.1 constant_dynamic-update-slice_fusion.2
  146.1 4.5 %collective-permute-done.5 = bf16[32,4,512]{2,1,0:T(4,128)(2,1)S(1)} collective-permute-done((bf16[32,4,512]{2,1,0:T(4,128)(2,1)S(1)}, bf16[32,4,512]{2,1,0:T(4,128)(2,1)S(1)}, u32[]{:S(2)}, u32[]{:S(2)}) %collective-permute-start.5) | collective-permute-done | bytes 131104 | tf_op jit(solution)/shard_map/return_owner/ppermute | solution.py:337
  150.6 0.1 constant_dynamic-update-slice_fusion.1
  150.7 1.4 collective-permute-done.6
  152.0 0.1 constant_dynamic-update-slice_fusion.late_ref
  152.1 0.0 all-to-all-done.3.second_ref
  152.1 1.1 slice.18
  153.2 0.1 reshape.40.early_ref
  153.3 7.4 %finish.1 = (f32[192,4,768]{2,1,0:T(4,128)}, bf16[2,1024,768]{2,1,0:T(8,128)(2,1)S(1)}) custom-call(s32[16,256]{1,0:T(8,128)S(1)} %table.1.table_ref, s32[2]{0:T(128)S(1)} %pad_add_fusion.place_ref, bf16[256,4,512]{2,1,0:T(4,128)(2,1)S(1)} %constant_dynamic-update-slice_fusion.late_ref, bf16[256,4,256]{2,1,0:T(4,128)(2,1)S(1)} %reshape.40.early_ref, ...), custom_call_target="tpu_custom_call" | custom-call | tf_op jit(solution)/shard_map/finish/finish/pallas_call | solution.py:254
  160.7 0.0 copy-start.1
  160.7 1.7 %copy-done.1 = bf16[2,1024,768]{2,1,0:T(8,128)(2,1)} copy-done((bf16[2,1024,768]{2,1,0:T(8,128)(2,1)}, bf16[2,1024,768]{2,1,0:T(8,128)(2,1)S(1)}, u32[]{:S(2)}) %copy-start.1) | copy-done | bytes 3145752
  (8 shorter events, 0.2 us)
Async XLA Ops:
  10.4 56.5 %all-to-all-start.1 = ((bf16[256,4,768]{2,1,0:T(4,128)(2,1)}), bf16[256,4,768]{2,1,0:T(4,128)(2,1)S(1)}, u32[]{:S(2)}, u32[]{:S(2)}) async-start(bf16[256,4,768]{2,1,0:T(4,128)(2,1)} %get-tuple-element.33), calls=%async_computation.1 | async-start | bytes 3145728 | tf_op jit(solution)/shard_map/gather_matrix/all_to_all | solution.py:355
  80.1 16.5 %collective-permute-start.7 = (bf16[32,4,256]{2,1,0:T(4,128)(2,1)S(1)}, bf16[32,4,256]{2,1,0:T(4,128)(2,1)S(1)}, u32[]{:S(2)}, u32[]{:S(2)}) collective-permute-start(bf16[32,4,256]{2,1,0:T(4,128)(2,1)S(1)} %get-tuple-element.54), channel_id=1, source_target_pairs={{0,1},{1,2},{2,3},{3,4},{4,5},{5,6},{6,7},{7,0},{8,9},{9,10},{10,1... | collective-permute-start | bytes 196616 | tf_op jit(solution)/shard_map/return_owner_early/ppermute | solution.py:337
  80.5 25.3 %all-to-all-start.2 = ((bf16[32,32,768]{2,1,0:T(8,128)(2,1)}), bf16[32,32,768]{2,1,0:T(8,128)(2,1)S(1)}, u32[]{:S(2)}, u32[]{:S(2)}) async-start(bf16[32,32,768]{2,1,0:T(8,128)(2,1)} %bitcast.3), calls=%async_computation.2 | async-start | bytes 3145728 | tf_op jit(solution)/shard_map/return_dp/all_to_all | solution.py:360
  85.6 11.0 %collective-permute-start.8 = (bf16[32,4,256]{2,1,0:T(4,128)(2,1)S(1)}, bf16[32,4,256]{2,1,0:T(4,128)(2,1)S(1)}, u32[]{:S(2)}, u32[]{:S(2)}) collective-permute-start(bf16[32,4,256]{2,1,0:T(4,128)(2,1)S(1)} %get-tuple-element.53), channel_id=1, source_target_pairs={{0,2},{1,3},{2,4},{3,5},{4,6},{5,7},{6,0},{7,1},{8,10},{9,11},{10,... | collective-permute-start | bytes 196616 | tf_op jit(solution)/shard_map/return_owner_early/ppermute | solution.py:337
  86.7 14.1 %collective-permute-start.9 = (bf16[32,4,256]{2,1,0:T(4,128)(2,1)S(1)}, bf16[32,4,256]{2,1,0:T(4,128)(2,1)S(1)}, u32[]{:S(2)}, u32[]{:S(2)}) collective-permute-start(bf16[32,4,256]{2,1,0:T(4,128)(2,1)S(1)} %get-tuple-element.52), channel_id=1, source_target_pairs={{0,3},{1,4},{2,5},{3,6},{4,7},{5,0},{6,1},{7,2},{8,11},{9,12},{10,... | collective-permute-start | bytes 196616 | tf_op jit(solution)/shard_map/return_owner_early/ppermute | solution.py:337
  87.9 12.9 %collective-permute-start.10 = (bf16[32,4,256]{2,1,0:T(4,128)(2,1)S(1)}, bf16[32,4,256]{2,1,0:T(4,128)(2,1)S(1)}, u32[]{:S(2)}, u32[]{:S(2)}) collective-permute-start(bf16[32,4,256]{2,1,0:T(4,128)(2,1)S(1)} %get-tuple-element.51), channel_id=1, source_target_pairs={{0,4},{1,5},{2,6},{3,7},{4,0},{5,1},{6,2},{7,3},{8,12},{9,13},{10,... | collective-permute-start | bytes 196616 | tf_op jit(solution)/shard_map/return_owner_early/ppermute | solution.py:337
  92.9 12.0 %collective-permute-start.11 = (bf16[32,4,256]{2,1,0:T(4,128)(2,1)S(1)}, bf16[32,4,256]{2,1,0:T(4,128)(2,1)S(1)}, u32[]{:S(2)}, u32[]{:S(2)}) collective-permute-start(bf16[32,4,256]{2,1,0:T(4,128)(2,1)S(1)} %get-tuple-element.50), channel_id=1, source_target_pairs={{0,5},{1,6},{2,7},{3,0},{4,1},{5,2},{6,3},{7,4},{8,13},{9,14},{10,... | collective-permute-start | bytes 196616 | tf_op jit(solution)/shard_map/return_owner_early/ppermute | solution.py:337
  96.6 8.3 %collective-permute-start.12 = (bf16[32,4,256]{2,1,0:T(4,128)(2,1)S(1)}, bf16[32,4,256]{2,1,0:T(4,128)(2,1)S(1)}, u32[]{:S(2)}, u32[]{:S(2)}) collective-permute-start(bf16[32,4,256]{2,1,0:T(4,128)(2,1)S(1)} %get-tuple-element.49), channel_id=1, source_target_pairs={{0,6},{1,7},{2,0},{3,1},{4,2},{5,3},{6,4},{7,5},{8,14},{9,15},{10,... | collective-permute-start | bytes 196616 | tf_op jit(solution)/shard_map/return_owner_early/ppermute | solution.py:337
  96.6 8.6 %collective-permute-start.13 = (bf16[32,4,256]{2,1,0:T(4,128)(2,1)S(1)}, bf16[32,4,256]{2,1,0:T(4,128)(2,1)S(1)}, u32[]{:S(2)}, u32[]{:S(2)}) collective-permute-start(bf16[32,4,256]{2,1,0:T(4,128)(2,1)S(1)} %get-tuple-element.48), channel_id=1, source_target_pairs={{0,7},{1,0},{2,1},{3,2},{4,3},{5,4},{6,5},{7,6},{8,15},{9,8},{10,9... | collective-permute-start | bytes 196616 | tf_op jit(solution)/shard_map/return_owner_early/ppermute | solution.py:337
  106.8 1.3 copy-start
  108.1 44.0 %all-to-all-start.3 = ((bf16[32,32,1024]{2,1,0:T(8,128)(2,1)}), bf16[32,32,1024]{2,1,0:T(8,128)(2,1)}, u32[]{:S(2)}, u32[]{:S(2)}) async-start(bf16[32,32,1024]{2,1,0:T(8,128)(2,1)} %copy-done), calls=%async_computation.3 | async-start | bytes 4194304 | tf_op jit(solution)/shard_map/second_matrix/all_to_all | solution.py:367
  117.0 13.2 %collective-permute-start = (bf16[32,4,512]{2,1,0:T(4,128)(2,1)S(1)}, bf16[32,4,512]{2,1,0:T(4,128)(2,1)S(1)}, u32[]{:S(2)}, u32[]{:S(2)}) collective-permute-start(bf16[32,4,512]{2,1,0:T(4,128)(2,1)S(1)} %get-tuple-element.47), channel_id=1, source_target_pairs={{0,1},{1,2},{2,3},{3,4},{4,5},{5,6},{6,7},{7,0},{8,9},{9,10},{10,1... | collective-permute-start | bytes 393224 | tf_op jit(solution)/shard_map/return_owner/ppermute | solution.py:337
  119.6 12.5 %collective-permute-start.1 = (bf16[32,4,512]{2,1,0:T(4,128)(2,1)S(1)}, bf16[32,4,512]{2,1,0:T(4,128)(2,1)S(1)}, u32[]{:S(2)}, u32[]{:S(2)}) collective-permute-start(bf16[32,4,512]{2,1,0:T(4,128)(2,1)S(1)} %get-tuple-element.46), channel_id=1, source_target_pairs={{0,2},{1,3},{2,4},{3,5},{4,6},{5,7},{6,0},{7,1},{8,10},{9,11},{10,... | collective-permute-start | bytes 393224 | tf_op jit(solution)/shard_map/return_owner/ppermute | solution.py:337
  121.8 20.7 %collective-permute-start.2 = (bf16[32,4,512]{2,1,0:T(4,128)(2,1)S(1)}, bf16[32,4,512]{2,1,0:T(4,128)(2,1)S(1)}, u32[]{:S(2)}, u32[]{:S(2)}) collective-permute-start(bf16[32,4,512]{2,1,0:T(4,128)(2,1)S(1)} %get-tuple-element.45), channel_id=1, source_target_pairs={{0,3},{1,4},{2,5},{3,6},{4,7},{5,0},{6,1},{7,2},{8,11},{9,12},{10,... | collective-permute-start | bytes 393224 | tf_op jit(solution)/shard_map/return_owner/ppermute | solution.py:337
  124.7 17.8 %collective-permute-start.3 = (bf16[32,4,512]{2,1,0:T(4,128)(2,1)S(1)}, bf16[32,4,512]{2,1,0:T(4,128)(2,1)S(1)}, u32[]{:S(2)}, u32[]{:S(2)}) collective-permute-start(bf16[32,4,512]{2,1,0:T(4,128)(2,1)S(1)} %get-tuple-element.44), channel_id=1, source_target_pairs={{0,4},{1,5},{2,6},{3,7},{4,0},{5,1},{6,2},{7,3},{8,12},{9,13},{10,... | collective-permute-start | bytes 393224 | tf_op jit(solution)/shard_map/return_owner/ppermute | solution.py:337
  127.2 18.8 %collective-permute-start.4 = (bf16[32,4,512]{2,1,0:T(4,128)(2,1)S(1)}, bf16[32,4,512]{2,1,0:T(4,128)(2,1)S(1)}, u32[]{:S(2)}, u32[]{:S(2)}) collective-permute-start(bf16[32,4,512]{2,1,0:T(4,128)(2,1)S(1)} %get-tuple-element.43), channel_id=1, source_target_pairs={{0,5},{1,6},{2,7},{3,0},{4,1},{5,2},{6,3},{7,4},{8,13},{9,14},{10,... | collective-permute-start | bytes 393224 | tf_op jit(solution)/shard_map/return_owner/ppermute | solution.py:337
  130.3 20.4 %collective-permute-start.5 = (bf16[32,4,512]{2,1,0:T(4,128)(2,1)S(1)}, bf16[32,4,512]{2,1,0:T(4,128)(2,1)S(1)}, u32[]{:S(2)}, u32[]{:S(2)}) collective-permute-start(bf16[32,4,512]{2,1,0:T(4,128)(2,1)S(1)} %get-tuple-element.42), channel_id=1, source_target_pairs={{0,6},{1,7},{2,0},{3,1},{4,2},{5,3},{6,4},{7,5},{8,14},{9,15},{10,... | collective-permute-start | bytes 393224 | tf_op jit(solution)/shard_map/return_owner/ppermute | solution.py:337
  132.1 19.9 %collective-permute-start.6 = (bf16[32,4,512]{2,1,0:T(4,128)(2,1)S(1)}, bf16[32,4,512]{2,1,0:T(4,128)(2,1)S(1)}, u32[]{:S(2)}, u32[]{:S(2)}) collective-permute-start(bf16[32,4,512]{2,1,0:T(4,128)(2,1)S(1)} %get-tuple-element.41), channel_id=1, source_target_pairs={{0,7},{1,0},{2,1},{3,2},{4,3},{5,4},{6,5},{7,6},{8,15},{9,8},{10,9... | collective-permute-start | bytes 393224 | tf_op jit(solution)/shard_map/return_owner/ppermute | solution.py:337
  160.7 1.7 %copy-start.1 = (bf16[2,1024,768]{2,1,0:T(8,128)(2,1)}, bf16[2,1024,768]{2,1,0:T(8,128)(2,1)S(1)}, u32[]{:S(2)}) copy-start(bf16[2,1024,768]{2,1,0:T(8,128)(2,1)S(1)} %get-tuple-element.40) | copy-start | bytes 9437188
where the time goes:
time: 163 us; the launch traced here: 162 us
  waiting for transfers between devices  66 us (40%)
  starting transfers between devices  56.7 us (35%)
  Pallas kernels  27.5 us (17%)
  local copies, waits for them, and re-layouts  10.6 us (7%)
    all_to_all x1, waiting for transfers between devices, shards(): received = lax.all_to_all(outgoing, ('dp', 'owner'), 0, 0, tiled=True)  42.1 us
    ppermute x14, starting transfers between devices, send_planes(): lax.ppermute(to_plane(far), 'owner', [(i, (i + far) % planes) for i in ra...  29.6 us
    ppermute x14, waiting for transfers between devices, send_planes(): lax.ppermute(to_plane(far), 'owner', [(i, (i + far) % planes) for i in ra...  23.5 us
    all_to_all x1, starting transfers between devices, shards(): received = lax.all_to_all(outgoing, ('dp', 'owner'), 0, 0, tiled=True)  14.4 us
    pallas_call x1, Pallas kernels, orthogonalize(): pl.pallas_call(functools.partial(orthogonalize_kernel, scale), out_shape=...  9.41 us
    pallas_call x1, Pallas kernels, momentum_step(): pl.pallas_call(momentum_kernel, grid_spec=pltpu.PrefetchScalarGridSpec(nu...  7.62 us
    all_to_all x1, starting transfers between devices, shards(): lax.all_to_all(pack(table, place, parts, early), 'dp', 0, 0, tiled=True)  7.6 us
    pallas_call x1, Pallas kernels, finish(): pl.pallas_call(finish_kernel, grid_spec=pltpu.PrefetchScalarGridSpec(num_...  7.41 us
  transfers between devices with their start and end apart: 17, of which 10 were waited for; matrix products, arithmetic and copies ran while one was open for 2% of the time, Pallas kernels for 0%

commit v1 on v0

v1 whole, which is shorter than its diff:
```python
import functools
import math

import jax
import jax.numpy as jnp
from jax import lax
from jax.experimental import pallas as pl
from jax.experimental.pallas import tpu as pltpu
from jax.sharding import PartitionSpec as P

ITERS = 2
CAP = 2

momentum_decay = 0.95
quintic_one = 3.4445
quintic_two = -4.775
quintic_three = 2.0315
norm_epsilon = 1e-07

SLOT, FIRST, SECOND, SPILLED, PART, MATRIX, HELPER_INDEX = range(7)
TABLE_ROWS = 8


def early_distances(planes):
    return [planes // 2 - 1, planes // 2 + 1]


def late_distances(planes):
    early = early_distances(planes)
    return sorted((far for far in range(1, planes) if far not in early), key=lambda far: -min(far, planes - far))


def distances(planes):
    return [0, *late_distances(planes), *early_distances(planes)]


def fill_table(planes, place_ref, owner_ref, table_ref):
    mats = owner_ref.shape[1]
    devices = table_ref.shape[1]
    f32 = jnp.float32

    def iota(rows, cols, axis):
        return lax.broadcasted_iota(jnp.int32, (rows, cols), axis)

    def total(cond, axis):
        return jnp.sum(jnp.where(cond, 1.0, 0.0).astype(f32), axis=axis, keepdims=True)

    def column(row):
        n = row.shape[1]
        return jnp.sum(jnp.where(iota(n, n, 0) == iota(n, n, 1), row, 0.0), axis=1, keepdims=True)

    own_row = owner_ref[...].astype(f32)
    own_col = column(own_row)
    same = own_col == own_row
    rank_row = total(same & (iota(mats, mats, 0) < iota(mats, mats, 1)), 0)
    rank_col = total(same & (iota(mats, mats, 1) < iota(mats, mats, 0)), 1)
    held = own_col == iota(mats, devices, 1).astype(f32)
    first_row = total(held & (rank_col == 0.0), 0)
    second_row = total(held & (rank_col == 1.0), 0)
    held = own_row == iota(devices, mats, 0).astype(f32)
    first_col = total(held & (rank_row == 0.0), 1)
    second_col = total(held & (rank_row == 1.0), 1)
    up, down = iota(devices, devices, 0), iota(devices, devices, 1)
    plane = (up & (planes - 1)) == (down & (planes - 1))
    before_row, before_col = up < down, down < up
    free_index = total(before_col & plane & (first_row == 0.0), 1)
    second_index = total(before_row & plane & (second_col == 1.0), 0)
    pair = plane & (first_col == 0.0) & (second_row == 1.0) & (free_index == second_index)
    left_row = second_row - total(pair, 0)
    idle_col = 1.0 - first_col - total(pair, 1)
    left_col = column(left_row)
    idle_row = jnp.sum(jnp.where(up == down, idle_col, 0.0), axis=0, keepdims=True)
    left_index = total(before_row & (left_col == 1.0), 0)
    idle_index = total(before_col & (idle_row == 1.0), 1)
    spill = (left_row == 1.0) & (idle_col == 1.0) & (left_index == idle_index)
    helper_row = jnp.sum(jnp.where(pair | spill, up.astype(f32), 0.0), axis=0, keepdims=True)
    helper_col = column(helper_row)
    helper_of = jnp.sum(jnp.where(held, helper_col, 0.0), axis=0, keepdims=True)
    slot_row = jnp.where(rank_row == 0.0, own_row, helper_of)
    spilled = jnp.sum(left_row, axis=1, keepdims=True)
    slot_row = slot_row.astype(jnp.int32)
    helper_row = helper_row.astype(jnp.int32)
    shift = planes.bit_length() - 1
    count = devices // planes

    order = distances(planes)

    def arrival(slot):
        far = (place_ref[0] - slot) & (planes - 1)
        position = sum(jnp.where(far == distance, i, 0) for i, distance in enumerate(order))
        return position * count + (slot >> shift)

    slot_col = column(slot_row.astype(f32)).astype(jnp.int32)
    lands = arrival(slot_col) == iota(mats, devices, 1)
    matrix_row = jnp.sum(jnp.where(lands, iota(mats, devices, 0) + 1, 0).astype(f32), axis=0, keepdims=True) - 1.0

    mine = up == (down * planes + place_ref[0])
    helper_here = column(helper_row.astype(f32))
    part_row = jnp.sum(jnp.where(mine, helper_here, 0.0), axis=0, keepdims=True).astype(jnp.int32) >> shift

    def put(row, values):
        table_ref[row : row + 1, : values.shape[1]] = values.astype(jnp.int32)

    table_ref[...] = jnp.zeros_like(table_ref)
    put(SLOT, slot_row)
    put(FIRST, first_row)
    put(SECOND, second_row)
    put(SPILLED, jnp.broadcast_to(spilled, (1, devices)))
    put(PART, part_row)
    put(MATRIX, matrix_row)
    put(HELPER_INDEX, arrival(helper_row))


def start_kernel(
    planes, place_ref, owner_ref, momentum_ref, grad_ref, table_ref, new_ref, out_ref, new, grad, slots, in_sem, out_sem, slot_sem
):
    chunks = in_sem.shape[1]
    block = new.shape[0] // chunks

    def part(chunk):
        return pl.ds(chunk * block, block)

    def copies_in(chunk):
        return (
            pltpu.make_async_copy(momentum_ref.at[part(chunk)], new.at[part(chunk)], in_sem.at[0, chunk]),
            pltpu.make_async_copy(grad_ref.at[part(chunk)], grad.at[part(chunk)], in_sem.at[1, chunk]),
        )

    def copy_out(chunk):
        return pltpu.make_async_copy(new.at[part(chunk)], new_ref.at[part(chunk)], out_sem.at[chunk])

    for chunk in range(chunks):
        for copy in copies_in(chunk):
            copy.start()
    fill_table(planes, place_ref, owner_ref, table_ref)
    slot_copy = pltpu.make_async_copy(table_ref.at[pl.ds(0, 8)], slots, slot_sem)
    slot_copy.start()
    out_ref[...] = jnp.zeros_like(out_ref)
    slot_copy.wait()

    def each(chunk, _):
        for copy in copies_in(chunk):
            copy.wait()
        for i in range(block):
            mat = chunk * block + i
            value = grad[mat].astype(jnp.float32)
            result = momentum_decay * new[mat] + value
            new[mat] = result
            out_ref[slots[SLOT, mat]] = (value + momentum_decay * result).astype(out_ref.dtype)
        copy_out(chunk).start()

    lax.fori_loop(0, chunks, each, None)
    for chunk in range(chunks):
        copy_out(chunk).wait()


def start(place, owner_table, momentum, grad, planes, devices, chunks=8):
    mats, rows, cols = momentum.shape
    while mats % chunks:
        chunks -= 1
    hbm = pl.BlockSpec(memory_space=pltpu.HBM)
    outgoing = (devices, rows, cols)
    return pl.pallas_call(
        functools.partial(start_kernel, planes),
        grid_spec=pltpu.PrefetchScalarGridSpec(
            num_scalar_prefetch=1,
            grid=(1,),
            in_specs=[pl.BlockSpec((1, mats), lambda *_: (0, 0)), hbm, hbm],
            out_specs=[
                pl.BlockSpec((TABLE_ROWS, devices), lambda *_: (0, 0)),
                hbm,
                pl.BlockSpec(outgoing, lambda *_: (0, 0, 0)),
            ],
            scratch_shapes=[
                pltpu.VMEM(momentum.shape, momentum.dtype),
                pltpu.VMEM(grad.shape, grad.dtype),
                pltpu.SMEM((8, devices), jnp.int32),
                pltpu.SemaphoreType.DMA((2, chunks)),
                pltpu.SemaphoreType.DMA((chunks,)),
                pltpu.SemaphoreType.DMA,
            ],
        ),
        out_shape=[
            jax.ShapeDtypeStruct((TABLE_ROWS, devices), jnp.int32),
            jax.ShapeDtypeStruct(momentum.shape, jnp.float32),
            jax.ShapeDtypeStruct(outgoing, jnp.bfloat16),
        ],
        compiler_params=pltpu.CompilerParams(vmem_limit_bytes=60 * 1024 * 1024),
        name="start",
    )(place, owner_table.reshape(1, mats), momentum, grad)


def orthogonalize_kernel(scale, x_ref, out_ref, again_ref, iterate_ref, gram_ref, poly_ref):
    rows, cols = x_ref.shape
    tile, side = min(256, rows), min(256, cols) if cols % 256 == 0 else 128
    f32, bf16 = jnp.float32, jnp.bfloat16
    starts = range(0, cols, side)

    def put(ref, i, block):
        ref[i : i + side, i:] = block
        for j in range(i + side, cols, side):
            ref[j : j + side, i : i + side] = block[:, j - i : j - i + side].T

    def gram_rows(ref, i):
        return lax.dot_general(ref[:, i : i + side], ref[:, i:], (((0,), (0,)), ((), ())), preferred_element_type=f32)

    def poly():
        for i in starts:
            square = jnp.dot(gram_ref[i : i + side, :], gram_ref[:, i:], preferred_element_type=f32)
            put(poly_ref, i, (quintic_two * gram_ref[i : i + side, i:].astype(f32) + quintic_three * square).astype(bf16))

    def apply(source_ref, target_ref, factor, last):
        for i in range(0, rows, tile):
            part = source_ref[i : i + tile, :]
            step = quintic_one * part.astype(f32) + jnp.dot(part, poly_ref[...], preferred_element_type=f32)
            step = (step * factor).astype(bf16) if factor is not None else step.astype(bf16)
            step = step * jnp.asarray(scale, bf16) if last else step
            target_ref[i : i + tile, :] = step
            if last:
                again_ref[i : i + tile, :] = step

    gram = [gram_rows(x_ref, i) for i in starts]
    diagonal = lax.broadcasted_iota(jnp.int32, (side, side), 0) == lax.broadcasted_iota(jnp.int32, (side, side), 1)
    squares = sum(jnp.where(diagonal, block[:, :side], 0.0) for block in gram)
    trace = jnp.sum(jnp.sum(squares, axis=0, keepdims=True), axis=1, keepdims=True)
    factor = 1.0 / (jnp.sqrt(trace) + norm_epsilon)
    for i, block in zip(starts, gram):
        put(gram_ref, i, (block * factor * factor).astype(bf16))
    poly()
    apply(x_ref, iterate_ref, factor, False)
    for step in range(1, ITERS):
        for i in starts:
            put(gram_ref, i, gram_rows(iterate_ref, i).astype(bf16))
        poly()
        apply(iterate_ref, out_ref, None, True)


def orthogonalize(matrix, scale):
    rows, cols = matrix.shape
    return pl.pallas_call(
        functools.partial(orthogonalize_kernel, scale),
        out_shape=[jax.ShapeDtypeStruct((rows, cols), jnp.bfloat16)] * 2,
        scratch_shapes=[
            pltpu.VMEM((rows, cols), jnp.bfloat16),
            pltpu.VMEM((cols, cols), jnp.bfloat16),
            pltpu.VMEM((cols, cols), jnp.bfloat16),
        ],
        compiler_params=pltpu.CompilerParams(vmem_limit_bytes=24 * 1024 * 1024),
        cost_estimate=pl.CostEstimate(flops=ITERS * 2 * cols * cols * (2 * rows + cols), bytes_accessed=4 * rows * cols, transcendentals=0),
        name="orthogonalize",
    )(matrix)


def pack_kernel(table_ref, parts_ref, early_ref, out_ref):
    count, rows, _ = parts_ref.shape
    out_ref[:, rows:, :] = early_ref[...]

    def each(i, _):
        out_ref[i, :rows, :] = parts_ref[table_ref[PART, i]]

    lax.fori_loop(0, count, each, None, unroll=True)


def pack(table, parts, early):
    count, rows, cols = parts.shape
    shape = (count, rows + early.shape[1], cols)
    return pl.pallas_call(
        pack_kernel,
        grid_spec=pltpu.PrefetchScalarGridSpec(
            num_scalar_prefetch=1,
            grid=(1,),
            in_specs=[pl.BlockSpec(x.shape, lambda *_: (0, 0, 0)) for x in (parts, early)],
            out_specs=pl.BlockSpec(shape, lambda *_: (0, 0, 0)),
        ),
        out_shape=jax.ShapeDtypeStruct(shape, parts.dtype),
        compiler_params=pltpu.CompilerParams(vmem_limit_bytes=14 * 1024 * 1024),
        name="pack",
    )(table, parts, early)


def spread(table_ref, first, pieces, staged_ref, update_ref, sem):
    for k, piece in enumerate(pieces):
        count = piece.shape[0]
        staged_ref[k * count : (k + 1) * count] = piece.astype(jnp.float32)

        def each(i, _, at=k * count):
            matrix = table_ref[MATRIX, first * count + at + i]

            @pl.when(matrix >= 0)
            def _():
                pltpu.make_async_copy(staged_ref.at[at + i], update_ref.at[matrix], sem).start()

        lax.fori_loop(0, count, each, None, unroll=8 if count % 8 == 0 else 1)


def finish_kernel(pieces, early, table_ref, place_ref, mine_ref, second_ref, *refs):
    pieces_refs, (update_ref, owned_ref, staged_ref, slots_ref, sem, slot_sem) = refs[:pieces], refs[pieces:]
    me = place_ref[1]
    count, rows, cols = pieces_refs[0].shape
    whole_rows = mine_ref.shape[0]
    mine = mine_ref[...]
    slots_ref[0] = jnp.where(table_ref[FIRST, me] > 0, mine, jnp.zeros_like(mine))
    keep = second_ref.shape[1] - early * rows
    second = second_ref[:, :keep, :].reshape(whole_rows, cols)
    slots_ref[1] = jnp.where(table_ref[SECOND, me] > 0, second, jnp.zeros_like(second))
    owned = pltpu.make_async_copy(slots_ref, owned_ref, slot_sem)
    owned.start()
    early_rows = second_ref[:, keep:, :].astype(jnp.float32)
    values = [ref[...] for ref in pieces_refs] + [early_rows[:, i * rows : (i + 1) * rows, :] for i in range(early)]
    spread(table_ref, 0, values, staged_ref, update_ref, sem)
    pltpu.make_async_copy(staged_ref.at[pl.ds(0, update_ref.shape[0])], update_ref, sem).wait()
    owned.wait()


def finish(table, place, late, mine, second, mats, early):
    count, rows, cols = late[0].shape
    hbm = pl.BlockSpec(memory_space=pltpu.HBM)

    def whole(x):
        return pl.BlockSpec(x.shape, lambda *_: (0,) * len(x.shape))

    owned_shape = (CAP, *mine.shape)
    return pl.pallas_call(
        functools.partial(finish_kernel, len(late), early),
        grid_spec=pltpu.PrefetchScalarGridSpec(
            num_scalar_prefetch=2,
            grid=(1,),
            in_specs=[whole(mine), whole(second), *(whole(piece) for piece in late)],
            out_specs=[hbm, hbm],
            scratch_shapes=[
                pltpu.VMEM(((len(late) + early) * count, rows, cols), jnp.float32),
                pltpu.VMEM(owned_shape, mine.dtype),
                pltpu.SemaphoreType.DMA,
                pltpu.SemaphoreType.DMA,
            ],
        ),
        out_shape=[
            jax.ShapeDtypeStruct((mats, rows, cols), jnp.float32),
            jax.ShapeDtypeStruct(owned_shape, mine.dtype),
        ],
        compiler_params=pltpu.CompilerParams(vmem_limit_bytes=32 * 1024 * 1024),
        name="finish",
    )(table, place, mine, second, *late)


def spilled_kernel(table_ref, arrived_ref, out_ref):
    def each(i, _):
        out_ref[i] = arrived_ref[table_ref[HELPER_INDEX, i]]

    lax.fori_loop(0, out_ref.shape[0], each, None)


def spilled_rows(table, arrived):
    whole = pl.BlockSpec(arrived.shape, lambda *_: (0, 0, 0))
    return pl.pallas_call(
        spilled_kernel,
        grid_spec=pltpu.PrefetchScalarGridSpec(num_scalar_prefetch=1, grid=(1,), in_specs=[whole], out_specs=whole),
        out_shape=jax.ShapeDtypeStruct(arrived.shape, arrived.dtype),
        compiler_params=pltpu.CompilerParams(vmem_limit_bytes=14 * 1024 * 1024),
        name="spilled",
    )(table, arrived)


def send_planes(rows, way):
    planes = lax.axis_size("owner")
    me = lax.axis_index("owner")
    arrived = []
    for far in way:
        piece = lax.dynamic_index_in_dim(rows, lax.rem(me + far, planes), 1, keepdims=False)
        arrived.append(lax.ppermute(piece, "owner", [(i, (i + far) % planes) for i in range(planes)]) if far else piece)
    return arrived


def shards(momentum, grad, owner_table):
    dp_count = lax.axis_size("dp")
    planes = lax.axis_size("owner")
    devices = dp_count * planes
    mats, rows, cols = momentum.shape
    whole_rows = devices * rows
    early_ways = early_distances(planes)
    my_plane = lax.axis_index("owner")
    place = jnp.stack([my_plane, lax.axis_index("dp") * planes + my_plane]).astype(jnp.int32)
    with jax.named_scope("start"):
        table, new_momentum, outgoing = start(place, owner_table, momentum, grad, planes, devices)
    with jax.named_scope("gather_matrix"):
        received = lax.all_to_all(outgoing, ("dp", "owner"), 0, 0, tiled=True)
        matrix = received.reshape(whole_rows, cols)
    with jax.named_scope("orthogonalize"):
        mine, again = orthogonalize(matrix, math.sqrt(whole_rows))
    with jax.named_scope("return_dp"):
        parts = lax.all_to_all(mine.reshape(dp_count, planes * rows, cols), "dp", 0, 0, tiled=True)
    with jax.named_scope("return_owner_early"):
        early = jnp.concatenate(send_planes(again.reshape(dp_count, planes, rows, cols), early_ways), 1)
    with jax.named_scope("return_owner"):
        late = send_planes(parts.reshape(dp_count, planes, rows, cols), [0, *late_distances(planes)])
    with jax.named_scope("second_matrix"):
        second = lax.all_to_all(pack(table, parts, early), "dp", 0, 0, tiled=True)

    def with_spilled(second, *late):
        came_early = second[:, planes * rows :].reshape(dp_count, len(early_ways), rows, cols)
        arrived = jnp.concatenate([*late, *(came_early[:, i] for i in range(len(early_ways)))])
        rows_out = lax.all_to_all(spilled_rows(table, arrived), ("dp", "owner"), 0, 0, tiled=True)
        return jnp.concatenate([rows_out.reshape(dp_count, planes * rows, cols), second[:, planes * rows :]], 1)

    with jax.named_scope("spilled"):
        second = lax.cond(table[SPILLED, 0] > 0, with_spilled, lambda second, *late: second, second, *late)
    with jax.named_scope("finish"):
        update, owned = finish(table, place, late, mine, second, mats, len(early_ways))
    return new_momentum, update, owned[:, None]


def solution(mesh):
    in_specs = (P(None, ("dp", "owner"), None), P(None, ("dp", "owner"), None), P())
    out_specs = (
        P(None, ("dp", "owner"), None),
        P(None, ("dp", "owner"), None),
        P(None, ("dp", "owner"), None, None),
    )
    return jax.shard_map(shards, mesh=mesh, in_specs=in_specs, out_specs=out_specs, check_vma=False)
```

time: 163 us -> 145 us (0.89)
  blocking collectives: 0 us -> 56.5 us
  waiting for transfers between devices: 66 us -> 28.9 us
  starting transfers between devices: 56.7 us -> 28.9 us
  Pallas kernels: 27.5 us -> 20.2 us
  local copies, waits for them, and re-layouts: 10.6 us -> 7.09 us
    all_to_all x0 -> x1, blocking collectives: none -> 56.5 us  [shards(): received = lax.all_to_all(outgoing, ('dp', 'owner'), 0, 0, tiled=True)]
    all_to_all x2 -> x1, waiting for transfers between devices: 42.1 us -> 0.01 us  [shards(): second = lax.all_to_all(pack(table, parts, early), 'dp', 0, 0, tiled=True)]
    all_to_all x2 -> x1, starting transfers between devices: 22 us -> 6.92 us  [shards(): second = lax.all_to_all(pack(table, parts, early), 'dp', 0, 0, tiled=True)]
    ppermute x14 -> x7, starting transfers between devices: 29.6 us -> 16.8 us  [send_planes(): lax.ppermute(piece, 'owner', [(i, (i + far) % planes) for i in range(plan...]
    pallas_call x3 -> x2, Pallas kernels: 17.1 us -> 11 us  [the longest x1 6.1 us: start(): pl.pallas_call(functools.partial(start_kernel, planes), grid_spec=pltpu.P...]
    ppermute x14 -> x7, waiting for transfers between devices: 23.5 us -> 27.8 us  [send_planes(): lax.ppermute(piece, 'owner', [(i, (i + far) % planes) for i in range(plan...]
    unnamed x17 -> x2, local copies, waits for them, and re-layouts: 3.6 us -> 0.61 us
    pallas_call x1, Pallas kernels: 9.41 us -> 7.19 us  [orthogonalize(): pl.pallas_call(functools.partial(orthogonalize_kernel, scale), out_shape=...]
  transfers between devices with their start and end apart: 17 -> 9, of which waited for: 10 -> 4; matrix products, arithmetic and copies ran while one was open for 2% -> 4% of each run, Pallas kernels for 0% -> 0%
where the time goes in v1:
time: 145 us; the launch traced here: 144 us
  blocking collectives  56.5 us (39%)
  starting transfers between devices  28.9 us (20%)
  waiting for transfers between devices  28.9 us (20%)
  Pallas kernels  20.2 us (14%)
  local copies, waits for them, and re-layouts  7.09 us (5%)
  between operations  1.58 us (1%)
    all_to_all x1, blocking collectives, shards(): received = lax.all_to_all(outgoing, ('dp', 'owner'), 0, 0, tiled=True)  56.5 us
    ppermute x7, waiting for transfers between devices, send_planes(): lax.ppermute(piece, 'owner', [(i, (i + far) % planes) for i in range(plan...  27.8 us
    ppermute x7, starting transfers between devices, send_planes(): lax.ppermute(piece, 'owner', [(i, (i + far) % planes) for i in range(plan...  16.8 us
    pallas_call x1, Pallas kernels, orthogonalize(): pl.pallas_call(functools.partial(orthogonalize_kernel, scale), out_shape=...  7.19 us
    all_to_all x1, starting transfers between devices, shards(): second = lax.all_to_all(pack(table, parts, early), 'dp', 0, 0, tiled=True)  6.92 us
    pallas_call x1, Pallas kernels, start(): pl.pallas_call(functools.partial(start_kernel, planes), grid_spec=pltpu.P...  6.1 us
    all_to_all x1, starting transfers between devices, shards(): lax.all_to_all(mine.reshape(dp_count, planes * rows, cols), 'dp', 0, 0, t...  5.12 us
    pallas_call x1, Pallas kernels, finish(): pl.pallas_call(functools.partial(finish_kernel, len(late), early), grid_s...  4.9 us
  transfers between devices with their start and end apart: 9, of which 4 were waited for; matrix products, arithmetic and copies ran while one was open for 4% of the time, Pallas kernels for 0%

profile of v1, /device:TPU:34, one launch (start us, length us, event | category | flops | bytes accessed | tf_op | source)
XLA Modules:
  0.0 144.0 jit_solution(9130825950407365055)
XLA Ops:
  0.6 0.6 pad_add_fusion.place_ref
  1.2 6.1 %start.1 = (s32[8,256]{1,0:T(8,128)S(1)}, f32[192,4,768]{2,1,0:T(4,128)}, bf16[256,4,768]{2,1,0:T(4,128)(2,1)}) custom-call(s32[2]{0:T(128)} %pad_add_fusion.place_ref, s32[1,192]{1,0:T(1,128)} %bitcast.50, f32[192,4,768]{2,1,0:T(4,128)} %momentum_ref.1, bf16[192,4,768]{2,1,0:T(4,128)(2,1)} %grad_ref.1), custom_call_target="tpu_custom_call" | custom-call | tf_op jit(solution)/shard_map/start/start/pallas_call | solution.py:163
  7.4 56.5 %all_to_all.22 = bf16[256,4,768]{2,1,0:T(4,128)(2,1)S(1)} all-to-all(bf16[256,4,768]{2,1,0:T(4,128)(2,1)} %get-tuple-element.40), channel_id=1, replica_groups=mesh['dp'=32,'owner'=8] {'dp','owner'}, dimensions={0} | all-to-all | bytes 3145728 | tf_op jit(solution)/shard_map/gather_matrix/all_to_all | solution.py:386
  63.9 0.4 reshape.32.x_ref
  64.2 7.2 %orthogonalize.1 = (bf16[1024,768]{1,0:T(8,128)(2,1)}, bf16[1024,768]{1,0:T(8,128)(2,1)S(1)}) custom-call(bf16[1024,768]{1,0:T(8,128)(2,1)S(1)} %reshape.32.x_ref), custom_call_target="tpu_custom_call" | custom-call | flops 6643777536 | bytes 3145728 | tf_op jit(solution)/shard_map/orthogonalize/orthogonalize/pallas_call | solution.py:240
  71.4 5.1 %all-to-all-start.2 = ((bf16[32,32,768]{2,1,0:T(8,128)(2,1)}), bf16[32,32,768]{2,1,0:T(8,128)(2,1)S(1)}, u32[]{:S(2)}, u32[]{:S(2)}) async-start(bf16[32,32,768]{2,1,0:T(8,128)(2,1)} %bitcast.7), calls=%async_computation.2 | async-start | bytes 3145728 | tf_op jit(solution)/shard_map/return_dp/all_to_all | solution.py:391
  76.6 1.3 reshape.34
  77.9 1.2 dynamic-slice_bitcast_fusion.7
  79.1 0.6 collective-permute-start
  79.7 4.5 %collective-permute-start.1 = (bf16[32,4,768]{2,1,0:T(4,128)(2,1)S(1)}, bf16[32,4,768]{2,1,0:T(4,128)(2,1)S(1)}, u32[]{:S(2)}, u32[]{:S(2)}) collective-permute-start(bf16[32,4,768]{2,1,0:T(4,128)(2,1)S(1)} %get-tuple-element.68), channel_id=1, source_target_pairs={{0,5},{1,6},{2,7},{3,0},{4,1},{5,2},{6,3},{7,4},{8,13},{9,14},{10,... | collective-permute-start | bytes 589832 | tf_op jit(solution)/shard_map/return_owner_early/ppermute | solution.py:370
  84.2 11.2 %collective-permute-done = bf16[32,4,768]{2,1,0:T(4,128)(2,1)S(1)} collective-permute-done((bf16[32,4,768]{2,1,0:T(4,128)(2,1)S(1)}, bf16[32,4,768]{2,1,0:T(4,128)(2,1)S(1)}, u32[]{:S(2)}, u32[]{:S(2)}) %collective-permute-start) | collective-permute-done | bytes 196640 | tf_op jit(solution)/shard_map/return_owner_early/ppermute | solution.py:370
  95.4 0.0 collective-permute-done.1
  95.4 0.2 pad_maximum_fusion.1.early_ref
  95.6 1.1 all-to-all-done.2.parts_ref
  96.8 2.1 %pack.1 = bf16[32,40,768]{2,1,0:T(8,128)(2,1)} custom-call(s32[8,256]{1,0:T(8,128)S(1)} %get-tuple-element.39.table_ref, bf16[32,32,768]{2,1,0:T(8,128)(2,1)S(1)} %all-to-all-done.2.parts_ref, bf16[32,8,768]{2,1,0:T(8,128)(2,1)S(1)} %pad_maximum_fusion.1.early_ref), custom_call_target="tpu_custom_call" | custom-call | tf_op jit(solution)/shard_map/second_matrix/pack/pallas_call | solution.py:267
  98.8 6.9 %all-to-all-start.3 = ((bf16[32,40,768]{2,1,0:T(8,128)(2,1)}), bf16[32,40,768]{2,1,0:T(8,128)(2,1)S(1)}, u32[]{:S(2)}, u32[]{:S(2)}) async-start(bf16[32,40,768]{2,1,0:T(8,128)(2,1)} %pack.1), calls=%async_computation.3 | async-start | bytes 3932160 | tf_op jit(solution)/shard_map/second_matrix/all_to_all | solution.py:397
  105.8 1.3 reshape.35
  107.1 1.8 %dynamic-slice_bitcast_fusion = (bf16[32,4,768]{2,1,0:T(4,128)(2,1)S(1)}, bf16[32,4,768]{2,1,0:T(4,128)(2,1)S(1)}, bf16[32,4,768]{2,1,0:T(4,128)(2,1)S(1)}, bf16...) fusion(bf16[32,8,4,768]{3,2,1,0:T(4,128)(2,1)} %reshape.35, ...), kind=kLoop, calls=%fused_computation.12 | loop fusion | bytes 2359320 | tf_op jit(solution)/shard_map/return_owner/jit(dynamic_index_in_dim)/squeeze | solution.py:369
  108.9 1.9 %collective-permute-start.6 = (bf16[32,4,768]{2,1,0:T(4,128)(2,1)S(1)}, bf16[32,4,768]{2,1,0:T(4,128)(2,1)S(1)}, u32[]{:S(2)}, u32[]{:S(2)}) collective-permute-start(bf16[32,4,768]{2,1,0:T(4,128)(2,1)S(1)} %get-tuple-element.61), channel_id=1, source_target_pairs={{0,7},{1,0},{2,1},{3,2},{4,3},{5,4},{6,5},{7,6},{8,15},{9,8},{10,9... | collective-permute-start | bytes 589832 | tf_op jit(solution)/shard_map/return_owner/ppermute | solution.py:370
  110.8 1.1 collective-permute-start.5
  111.8 4.9 %collective-permute-start.4 = (bf16[32,4,768]{2,1,0:T(4,128)(2,1)S(1)}, bf16[32,4,768]{2,1,0:T(4,128)(2,1)}, u32[]{:S(2)}, u32[]{:S(2)}) collective-permute-start(bf16[32,4,768]{2,1,0:T(4,128)(2,1)S(1)} %get-tuple-element.63), channel_id=1, source_target_pairs={{0,6},{1,7},{2,0},{3,1},{4,2},{5,3},{6,4},{7,5},{8,14},{9,15},{10,... | collective-permute-start | bytes 589832 | tf_op jit(solution)/shard_map/return_owner/ppermute | solution.py:370
  116.7 0.0 collective-permute-start.3
  116.7 3.9 %collective-permute-start.2 = (bf16[32,4,768]{2,1,0:T(4,128)(2,1)S(1)}, bf16[32,4,768]{2,1,0:T(4,128)(2,1)}, u32[]{:S(2)}, u32[]{:S(2)}) collective-permute-start(bf16[32,4,768]{2,1,0:T(4,128)(2,1)S(1)} %get-tuple-element.65), channel_id=1, source_target_pairs={{0,4},{1,5},{2,6},{3,7},{4,0},{5,1},{6,2},{7,3},{8,12},{9,13},{10,... | collective-permute-start | bytes 589832 | tf_op jit(solution)/shard_map/return_owner/ppermute | solution.py:370
  120.6 0.5 slice.13
  121.8 0.0 collective-permute-done.6.refs_5_
  121.8 0.0 collective-permute-done.5.refs_4_
  121.8 6.2 %collective-permute-done.4.refs_3_ = bf16[32,4,768]{2,1,0:T(4,128)(2,1)} collective-permute-done((bf16[32,4,768]{2,1,0:T(4,128)(2,1)S(1)}, bf16[32,4,768]{2,1,0:T(4,128)(2,1)}, u32[]{:S(2)}, u32[]{:S(2)}) %collective-permute-start.4) | collective-permute-done | bytes 196640 | tf_op jit(solution)/shard_map/return_owner/ppermute | solution.py:370
  128.0 10.4 %collective-permute-done.3.refs_2_ = bf16[32,4,768]{2,1,0:T(4,128)(2,1)} collective-permute-done((bf16[32,4,768]{2,1,0:T(4,128)(2,1)S(1)}, bf16[32,4,768]{2,1,0:T(4,128)(2,1)}, u32[]{:S(2)}, u32[]{:S(2)}) %collective-permute-start.3) | collective-permute-done | bytes 196640 | tf_op jit(solution)/shard_map/return_owner/ppermute | solution.py:370
  138.4 0.0 collective-permute-done.2.refs_1_
  138.4 0.0 all-to-all-done.3
  138.4 0.0 copy-start
  138.4 0.6 copy-done
  139.0 4.9 %finish.1 = (f32[192,4,768]{2,1,0:T(4,128)}, bf16[2,1024,768]{2,1,0:T(8,128)(2,1)}) custom-call(s32[8,256]{1,0:T(8,128)S(1)} %get-tuple-element.39.table_ref, s32[2]{0:T(128)S(1)} %copy-done, bf16[1024,768]{1,0:T(8,128)(2,1)} %get-tuple-element.41.mine_ref, bf16[32,40,768]{2,1,0:T(8,128)(2,1)S(1)} %get-tuple-element.69.second_ref, ...), custom_call_target="tpu_custom_call" | custom-call | tf_op jit(solution)/shard_map/finish/finish/pallas_call | solution.py:323
  (1 shorter events, 0.0 us)
Async XLA Ops:
  71.4 25.3 %all-to-all-start.2 = ((bf16[32,32,768]{2,1,0:T(8,128)(2,1)}), bf16[32,32,768]{2,1,0:T(8,128)(2,1)S(1)}, u32[]{:S(2)}, u32[]{:S(2)}) async-start(bf16[32,32,768]{2,1,0:T(8,128)(2,1)} %bitcast.7), calls=%async_computation.2 | async-start | bytes 3145728 | tf_op jit(solution)/shard_map/return_dp/all_to_all | solution.py:391
  79.1 16.3 %collective-permute-start = (bf16[32,4,768]{2,1,0:T(4,128)(2,1)S(1)}, bf16[32,4,768]{2,1,0:T(4,128)(2,1)S(1)}, u32[]{:S(2)}, u32[]{:S(2)}) collective-permute-start(bf16[32,4,768]{2,1,0:T(4,128)(2,1)S(1)} %get-tuple-element.67), channel_id=1, source_target_pairs={{0,3},{1,4},{2,5},{3,6},{4,7},{5,0},{6,1},{7,2},{8,11},{9,12},{10,... | collective-permute-start | bytes 589832 | tf_op jit(solution)/shard_map/return_owner_early/ppermute | solution.py:370
  79.7 15.7 %collective-permute-start.1 = (bf16[32,4,768]{2,1,0:T(4,128)(2,1)S(1)}, bf16[32,4,768]{2,1,0:T(4,128)(2,1)S(1)}, u32[]{:S(2)}, u32[]{:S(2)}) collective-permute-start(bf16[32,4,768]{2,1,0:T(4,128)(2,1)S(1)} %get-tuple-element.68), channel_id=1, source_target_pairs={{0,5},{1,6},{2,7},{3,0},{4,1},{5,2},{6,3},{7,4},{8,13},{9,14},{10,... | collective-permute-start | bytes 589832 | tf_op jit(solution)/shard_map/return_owner_early/ppermute | solution.py:370
  98.8 39.5 %all-to-all-start.3 = ((bf16[32,40,768]{2,1,0:T(8,128)(2,1)}), bf16[32,40,768]{2,1,0:T(8,128)(2,1)S(1)}, u32[]{:S(2)}, u32[]{:S(2)}) async-start(bf16[32,40,768]{2,1,0:T(8,128)(2,1)} %pack.1), calls=%async_computation.3 | async-start | bytes 3932160 | tf_op jit(solution)/shard_map/second_matrix/all_to_all | solution.py:397
  108.9 12.9 %collective-permute-start.6 = (bf16[32,4,768]{2,1,0:T(4,128)(2,1)S(1)}, bf16[32,4,768]{2,1,0:T(4,128)(2,1)S(1)}, u32[]{:S(2)}, u32[]{:S(2)}) collective-permute-start(bf16[32,4,768]{2,1,0:T(4,128)(2,1)S(1)} %get-tuple-element.61), channel_id=1, source_target_pairs={{0,7},{1,0},{2,1},{3,2},{4,3},{5,4},{6,5},{7,6},{8,15},{9,8},{10,9... | collective-permute-start | bytes 589832 | tf_op jit(solution)/shard_map/return_owner/ppermute | solution.py:370
  110.8 11.0 %collective-permute-start.5 = (bf16[32,4,768]{2,1,0:T(4,128)(2,1)S(1)}, bf16[32,4,768]{2,1,0:T(4,128)(2,1)S(1)}, u32[]{:S(2)}, u32[]{:S(2)}) collective-permute-start(bf16[32,4,768]{2,1,0:T(4,128)(2,1)S(1)} %get-tuple-element.62), channel_id=1, source_target_pairs={{0,1},{1,2},{2,3},{3,4},{4,5},{5,6},{6,7},{7,0},{8,9},{9,10},{10,1... | collective-permute-start | bytes 589832 | tf_op jit(solution)/shard_map/return_owner/ppermute | solution.py:370
  111.8 16.1 %collective-permute-start.4 = (bf16[32,4,768]{2,1,0:T(4,128)(2,1)S(1)}, bf16[32,4,768]{2,1,0:T(4,128)(2,1)}, u32[]{:S(2)}, u32[]{:S(2)}) collective-permute-start(bf16[32,4,768]{2,1,0:T(4,128)(2,1)S(1)} %get-tuple-element.63), channel_id=1, source_target_pairs={{0,6},{1,7},{2,0},{3,1},{4,2},{5,3},{6,4},{7,5},{8,14},{9,15},{10,... | collective-permute-start | bytes 589832 | tf_op jit(solution)/shard_map/return_owner/ppermute | solution.py:370
  116.7 21.6 %collective-permute-start.3 = (bf16[32,4,768]{2,1,0:T(4,128)(2,1)S(1)}, bf16[32,4,768]{2,1,0:T(4,128)(2,1)}, u32[]{:S(2)}, u32[]{:S(2)}) collective-permute-start(bf16[32,4,768]{2,1,0:T(4,128)(2,1)S(1)} %get-tuple-element.64), channel_id=1, source_target_pairs={{0,2},{1,3},{2,4},{3,5},{4,6},{5,7},{6,0},{7,1},{8,10},{9,11},{10,... | collective-permute-start | bytes 589832 | tf_op jit(solution)/shard_map/return_owner/ppermute | solution.py:370
  116.7 21.6 %collective-permute-start.2 = (bf16[32,4,768]{2,1,0:T(4,128)(2,1)S(1)}, bf16[32,4,768]{2,1,0:T(4,128)(2,1)}, u32[]{:S(2)}, u32[]{:S(2)}) collective-permute-start(bf16[32,4,768]{2,1,0:T(4,128)(2,1)S(1)} %get-tuple-element.65), channel_id=1, source_target_pairs={{0,4},{1,5},{2,6},{3,7},{4,0},{5,1},{6,2},{7,3},{8,12},{9,13},{10,... | collective-permute-start | bytes 589832 | tf_op jit(solution)/shard_map/return_owner/ppermute | solution.py:370
  138.4 0.6 copy-start

commit v2 on v1

--- a/solution.py
+++ b/solution.py
@@ -34,9 +34,10 @@
     return [0, *late_distances(planes), *early_distances(planes)]
 
 
-def fill_table(planes, place_ref, owner_ref, table_ref):
+def fill_table(planes, owner_ref, table_ref):
     mats = owner_ref.shape[1]
     devices = table_ref.shape[1]
+    my_plane = lax.axis_index("owner")
     f32 = jnp.float32
 
     def iota(rows, cols, axis):
@@ -86,7 +87,7 @@
     order = distances(planes)
 
     def arrival(slot):
-        far = (place_ref[0] - slot) & (planes - 1)
+        far = (my_plane - slot) & (planes - 1)
         position = sum(jnp.where(far == distance, i, 0) for i, distance in enumerate(order))
         return position * count + (slot >> shift)
 
@@ -94,7 +95,7 @@
     lands = arrival(slot_col) == iota(mats, devices, 1)
     matrix_row = jnp.sum(jnp.where(lands, iota(mats, devices, 0) + 1, 0).astype(f32), axis=0, keepdims=True) - 1.0
 
-    mine = up == (down * planes + place_ref[0])
+    mine = up == (down * planes + my_plane)
     helper_here = column(helper_row.astype(f32))
     part_row = jnp.sum(jnp.where(mine, helper_here, 0.0), axis=0, keepdims=True).astype(jnp.int32) >> shift
 
@@ -112,7 +113,7 @@
 
 
 def start_kernel(
-    planes, place_ref, owner_ref, momentum_ref, grad_ref, table_ref, new_ref, out_ref, new, grad, slots, in_sem, out_sem, slot_sem
+    planes, owner_ref, momentum_ref, grad_ref, table_ref, new_ref, out_ref, new, grad, slots, in_sem, out_sem, slot_sem
 ):
     chunks = in_sem.shape[1]
     block = new.shape[0] // chunks
@@ -132,10 +133,9 @@
     for chunk in range(chunks):
         for copy in copies_in(chunk):
             copy.start()
-    fill_table(planes, place_ref, owner_ref, table_ref)
+    fill_table(planes, owner_ref, table_ref)
     slot_copy = pltpu.make_async_copy(table_ref.at[pl.ds(0, 8)], slots, slot_sem)
     slot_copy.start()
-    out_ref[...] = jnp.zeros_like(out_ref)
     slot_copy.wait()
 
     def each(chunk, _):
@@ -154,7 +154,7 @@
         copy_out(chunk).wait()
 
 
-def start(place, owner_table, momentum, grad, planes, devices, chunks=8):
+def start(owner_table, momentum, grad, planes, devices, chunks=8):
     mats, rows, cols = momentum.shape
     while mats % chunks:
         chunks -= 1
@@ -163,7 +163,7 @@
     return pl.pallas_call(
         functools.partial(start_kernel, planes),
         grid_spec=pltpu.PrefetchScalarGridSpec(
-            num_scalar_prefetch=1,
+            num_scalar_prefetch=0,
             grid=(1,),
             in_specs=[pl.BlockSpec((1, mats), lambda *_: (0, 0)), hbm, hbm],
             out_specs=[
@@ -187,7 +187,7 @@
         ],
         compiler_params=pltpu.CompilerParams(vmem_limit_bytes=60 * 1024 * 1024),
         name="start",
-    )(place, owner_table.reshape(1, mats), momentum, grad)
+    )(owner_table.reshape(1, mats), momentum, grad)
 
 
 def orthogonalize_kernel(scale, x_ref, out_ref, again_ref, iterate_ref, gram_ref, poly_ref):
@@ -251,96 +251,113 @@
     )(matrix)
 
 
-def pack_kernel(table_ref, parts_ref, early_ref, out_ref):
-    count, rows, _ = parts_ref.shape
-    out_ref[:, rows:, :] = early_ref[...]
-
-    def each(i, _):
-        out_ref[i, :rows, :] = parts_ref[table_ref[PART, i]]
-
-    lax.fori_loop(0, count, each, None, unroll=True)
-
-
-def pack(table, parts, early):
-    count, rows, cols = parts.shape
-    shape = (count, rows + early.shape[1], cols)
+def pack_kernel(table_ref, parts_ref, *refs):
+    early_refs, out_ref = refs[:-1], refs[-1]
+    block = out_ref.shape[0]
+    groups = parts_ref.shape[1]
+    first = pl.program_id(0) * block
+    for k, early_ref in enumerate(early_refs):
+        out_ref[:, groups + k] = early_ref[...]
+    for i in range(block):
+        out_ref[i, :groups] = parts_ref[table_ref[PART, first + i]]
+
+
+def pack(table, parts, early, steps=4):
+    count, groups, rows, cols = parts.shape
+    block = count // steps
+    shape = (count, groups + len(early), rows, cols)
     return pl.pallas_call(
         pack_kernel,
         grid_spec=pltpu.PrefetchScalarGridSpec(
             num_scalar_prefetch=1,
-            grid=(1,),
-            in_specs=[pl.BlockSpec(x.shape, lambda *_: (0, 0, 0)) for x in (parts, early)],
-            out_specs=pl.BlockSpec(shape, lambda *_: (0, 0, 0)),
+            grid=(steps,),
+            in_specs=[
+                pl.BlockSpec(parts.shape, lambda i, *_: (0, 0, 0, 0)),
+                *(pl.BlockSpec((block, rows, cols), lambda i, *_: (i, 0, 0)) for _ in early),
+            ],
+            out_specs=pl.BlockSpec((block, *shape[1:]), lambda i, *_: (i, 0, 0, 0)),
         ),
         out_shape=jax.ShapeDtypeStruct(shape, parts.dtype),
         compiler_params=pltpu.CompilerParams(vmem_limit_bytes=14 * 1024 * 1024),
         name="pack",
-    )(table, parts, early)
-
-
-def spread(table_ref, first, pieces, staged_ref, update_ref, sem):
+    )(table, parts, *early)
+
+
+def finish_kernel(late, table_ref, mine_ref, second_ref, early_ref, *refs):
+    late_refs, (update_ref, owned_ref, staged_ref, zero_ref, sem, owned_sem) = refs[:late], refs[late:]
+    me = lax.axis_index("dp") * lax.axis_size("owner") + lax.axis_index("owner")
+    tile = zero_ref.shape[0]
+    zero_ref[...] = jnp.zeros_like(zero_ref)
+
+    def owned(act):
+        for slot, source_ref in enumerate((mine_ref, second_ref)):
+            present = table_ref[FIRST + slot, me] > 0
+
+            @pl.when(present)
+            def _():
+                act(pltpu.make_async_copy(source_ref, owned_ref.at[slot], owned_sem.at[slot, 0]))
+
+            @pl.when(jnp.logical_not(present))
+            def _():
+                for i in range(source_ref.shape[0] // tile):
+                    to_ref = owned_ref.at[slot, pl.ds(i * tile, tile)]
+                    act(pltpu.make_async_copy(zero_ref, to_ref, owned_sem.at[slot, i]))
+
+    owned(lambda copy: copy.start())
+    count = early_ref.shape[0]
+    pieces = [lambda ref=ref: ref[...] for ref in late_refs]
+    pieces += [lambda k=k: early_ref[:, k] for k in range(early_ref.shape[1])]
     for k, piece in enumerate(pieces):
-        count = piece.shape[0]
-        staged_ref[k * count : (k + 1) * count] = piece.astype(jnp.float32)
+        staged_ref[k * count : (k + 1) * count] = piece().astype(jnp.float32)
 
         def each(i, _, at=k * count):
-            matrix = table_ref[MATRIX, first * count + at + i]
+            matrix = table_ref[MATRIX, at + i]
 
             @pl.when(matrix >= 0)
             def _():
                 pltpu.make_async_copy(staged_ref.at[at + i], update_ref.at[matrix], sem).start()
 
         lax.fori_loop(0, count, each, None, unroll=8 if count % 8 == 0 else 1)
-
-
-def finish_kernel(pieces, early, table_ref, place_ref, mine_ref, second_ref, *refs):
-    pieces_refs, (update_ref, owned_ref, staged_ref, slots_ref, sem, slot_sem) = refs[:pieces], refs[pieces:]
-    me = place_ref[1]
-    count, rows, cols = pieces_refs[0].shape
-    whole_rows = mine_ref.shape[0]
-    mine = mine_ref[...]
-    slots_ref[0] = jnp.where(table_ref[FIRST, me] > 0, mine, jnp.zeros_like(mine))
-    keep = second_ref.shape[1] - early * rows
-    second = second_ref[:, :keep, :].reshape(whole_rows, cols)
-    slots_ref[1] = jnp.where(table_ref[SECOND, me] > 0, second, jnp.zeros_like(second))
-    owned = pltpu.make_async_copy(slots_ref, owned_ref, slot_sem)
-    owned.start()
-    early_rows = second_ref[:, keep:, :].astype(jnp.float32)
-    values = [ref[...] for ref in pieces_refs] + [early_rows[:, i * rows : (i + 1) * rows, :] for i in range(early)]
-    spread(table_ref, 0, values, staged_ref, update_ref, sem)
     pltpu.make_async_copy(staged_ref.at[pl.ds(0, update_ref.shape[0])], update_ref, sem).wait()
-    owned.wait()
-
-
-def finish(table, place, late, mine, second, mats, early):
+    owned(lambda copy: copy.wait())
+
+
+def finish(table, late, mine, second, packed, mats):
     count, rows, cols = late[0].shape
+    groups, early = packed.shape[1], packed.shape[1] - second.shape[0] // (count * rows)
     hbm = pl.BlockSpec(memory_space=pltpu.HBM)
+    tile = min(256, mine.shape[0])
 
     def whole(x):
         return pl.BlockSpec(x.shape, lambda *_: (0,) * len(x.shape))
 
     owned_shape = (CAP, *mine.shape)
     return pl.pallas_call(
-        functools.partial(finish_kernel, len(late), early),
+        functools.partial(finish_kernel, len(late)),
         grid_spec=pltpu.PrefetchScalarGridSpec(
-            num_scalar_prefetch=2,
+            num_scalar_prefetch=1,
             grid=(1,),
-            in_specs=[whole(mine), whole(second), *(whole(piece) for piece in late)],
+            in_specs=[
+                whole(mine),
+                whole(second),
+                pl.BlockSpec((count, early, rows, cols), lambda *_: (0, groups // early - 1, 0, 0)),
+                *(whole(piece) for piece in late),
+            ],
             out_specs=[hbm, hbm],
             scratch_shapes=[
                 pltpu.VMEM(((len(late) + early) * count, rows, cols), jnp.float32),
-                pltpu.VMEM(owned_shape, mine.dtype),
+                pltpu.VMEM((tile, cols), mine.dtype),
                 pltpu.SemaphoreType.DMA,
-                pltpu.SemaphoreType.DMA,
+                pltpu.SemaphoreType.DMA((CAP, mine.shape[0] // tile)),
             ],
         ),
         out_shape=[
             jax.ShapeDtypeStruct((mats, rows, cols), jnp.float32),
             jax.ShapeDtypeStruct(owned_shape, mine.dtype),
         ],
-        compiler_params=pltpu.CompilerParams(vmem_limit_bytes=32 * 1024 * 1024),
+        compiler_params=pltpu.CompilerParams(vmem_limit_bytes=24 * 1024 * 1024),
         name="finish",
-    )(table, place, mine, second, *late)
+    )(table, mine, second, packed, *late)
 
 
 def spilled_kernel(table_ref, arrived_ref, out_ref):
@@ -377,35 +394,34 @@
     devices = dp_count * planes
     mats, rows, cols = momentum.shape
     whole_rows = devices * rows
-    early_ways = early_distances(planes)
-    my_plane = lax.axis_index("owner")
-    place = jnp.stack([my_plane, lax.axis_index("dp") * planes + my_plane]).astype(jnp.int32)
     with jax.named_scope("start"):
-        table, new_momentum, outgoing = start(place, owner_table, momentum, grad, planes, devices)
+        table, new_momentum, outgoing = start(owner_table, momentum, grad, planes, devices)
     with jax.named_scope("gather_matrix"):
         received = lax.all_to_all(outgoing, ("dp", "owner"), 0, 0, tiled=True)
         matrix = received.reshape(whole_rows, cols)
     with jax.named_scope("orthogonalize"):
         mine, again = orthogonalize(matrix, math.sqrt(whole_rows))
     with jax.named_scope("return_dp"):
-        parts = lax.all_to_all(mine.reshape(dp_count, planes * rows, cols), "dp", 0, 0, tiled=True)
+        groups = again.reshape(dp_count, planes, rows, cols)
+        parts = lax.all_to_all(groups, "dp", 0, 0, tiled=True)
     with jax.named_scope("return_owner_early"):
-        early = jnp.concatenate(send_planes(again.reshape(dp_count, planes, rows, cols), early_ways), 1)
+        early = send_planes(groups, early_distances(planes))
     with jax.named_scope("return_owner"):
-        late = send_planes(parts.reshape(dp_count, planes, rows, cols), [0, *late_distances(planes)])
+        late = send_planes(parts, [0, *late_distances(planes)])
     with jax.named_scope("second_matrix"):
-        second = lax.all_to_all(pack(table, parts, early), "dp", 0, 0, tiled=True)
-
-    def with_spilled(second, *late):
-        came_early = second[:, planes * rows :].reshape(dp_count, len(early_ways), rows, cols)
-        arrived = jnp.concatenate([*late, *(came_early[:, i] for i in range(len(early_ways)))])
+        packed = lax.all_to_all(pack(table, parts, early), "dp", 0, 0, tiled=True)
+        second = packed[:, :planes].reshape(whole_rows, cols)
+
+    def with_spilled(second, packed, *late):
+        arrived = jnp.concatenate([*late, *(packed[:, planes + i] for i in range(len(early)))])
         rows_out = lax.all_to_all(spilled_rows(table, arrived), ("dp", "owner"), 0, 0, tiled=True)
-        return jnp.concatenate([rows_out.reshape(dp_count, planes * rows, cols), second[:, planes * rows :]], 1)
+        return rows_out.reshape(whole_rows, cols)
 
     with jax.named_scope("spilled"):
-        second = lax.cond(table[SPILLED, 0] > 0, with_spilled, lambda second, *late: second, second, *late)
+        spilled = table[SPILLED, 0] > 0
+        second = lax.cond(spilled, with_spilled, lambda second, *_: second, second, packed, *late)
     with jax.named_scope("finish"):
-        update, owned = finish(table, place, late, mine, second, mats, len(early_ways))
+        update, owned = finish(table, late, mine, second, packed, mats)
     return new_momentum, update, owned[:, None]
 
 

time: 145 us -> 146 us (level)
  local copies, waits for them, and re-layouts: 7.09 us -> 12.1 us
  starting transfers between devices: 28.9 us -> 25.2 us
  waiting for transfers between devices: 28.9 us -> 31.7 us
  Pallas kernels: 20.2 us -> 18.6 us
    ppermute x7, starting transfers between devices: 16.8 us -> 13.2 us  [send_planes(): lax.ppermute(piece, 'owner', [(i, (i + far) % planes) for i in range(plan...]
    ppermute x7, waiting for transfers between devices: 27.8 us -> 31.1 us  [send_planes(): lax.ppermute(piece, 'owner', [(i, (i + far) % planes) for i in range(plan...]
    reshape x2, local copies, waits for them, and re-layouts: 2.68 us -> 5.04 us  [the longest x1 3.72 us: shards(): second = packed[:, :planes].reshape(whole_rows, cols)]
    slice x1 -> x2, local copies, waits for them, and re-layouts: 0.51 us -> 2.49 us  [the longest x1 1.98 us: shards(): second = packed[:, :planes].reshape(whole_rows, cols)]
  transfers between devices with their start and end apart: 9 -> 9, of which waited for: 4 -> 7; matrix products, arithmetic and copies ran while one was open for 4% -> 2% of each run, Pallas kernels for 0% -> 0%
where the time goes in v2:
time: 146 us
  blocking collectives  56.5 us (39%)
  waiting for transfers between devices  31.7 us (22%)
  starting transfers between devices  25.2 us (17%)
  Pallas kernels  18.6 us (13%)
  local copies, waits for them, and re-layouts  12.1 us (8%)
  between operations  1.5 us (1%)
    all_to_all x1, blocking collectives, shards(): received = lax.all_to_all(outgoing, ('dp', 'owner'), 0, 0, tiled=True)  56.5 us
    ppermute x7, waiting for transfers between devices, send_planes(): lax.ppermute(piece, 'owner', [(i, (i + far) % planes) for i in range(plan...  31.1 us
    ppermute x7, starting transfers between devices, send_planes(): lax.ppermute(piece, 'owner', [(i, (i + far) % planes) for i in range(plan...  13.2 us
    all_to_all x1, starting transfers between devices, shards(): packed = lax.all_to_all(pack(table, parts, early), 'dp', 0, 0, tiled=True)  6.91 us
    pallas_call x1, Pallas kernels, orthogonalize(): pl.pallas_call(functools.partial(orthogonalize_kernel, scale), out_shape=...  6.02 us
    pallas_call x1, Pallas kernels, start(): pl.pallas_call(functools.partial(start_kernel, planes), grid_spec=pltpu.P...  5.19 us
    all_to_all x1, starting transfers between devices, shards(): parts = lax.all_to_all(groups, 'dp', 0, 0, tiled=True)  5.12 us
    pallas_call x1, Pallas kernels, finish(): pl.pallas_call(functools.partial(finish_kernel, len(late)), grid_spec=plt...  4.92 us
  transfers between devices with their start and end apart: 9, of which 7 were waited for; matrix products, arithmetic and copies ran while one was open for 2% of the time, Pallas kernels for 0%

profile of v2, /device:TPU:34, one launch (start us, length us, event | category | flops | bytes accessed | tf_op | source)
XLA Modules:
  0.0 145.7 jit_solution(10896903180795808431)
XLA Ops:
  0.6 5.2 %start.1 = (s32[8,256]{1,0:T(8,128)S(1)}, f32[192,4,768]{2,1,0:T(4,128)}, bf16[256,4,768]{2,1,0:T(4,128)(2,1)}) custom-call(s32[1,192]{1,0:T(1,128)} %bitcast.29, f32[192,4,768]{2,1,0:T(4,128)} %momentum_ref.1, bf16[192,4,768]{2,1,0:T(4,128)(2,1)} %grad_ref.1), custom_call_target="tpu_custom_call" | custom-call | tf_op jit(solution)/shard_map/start/start/pallas_call | solution.py:163
  5.8 56.5 %all_to_all.21 = bf16[256,4,768]{2,1,0:T(4,128)(2,1)S(1)} all-to-all(bf16[256,4,768]{2,1,0:T(4,128)(2,1)} %get-tuple-element.43), channel_id=1, replica_groups=mesh['dp'=32,'owner'=8] {'dp','owner'}, dimensions={0} | all-to-all | bytes 3145728 | tf_op jit(solution)/shard_map/gather_matrix/all_to_all | solution.py:400
  62.3 0.4 reshape.29.x_ref
  62.7 6.0 %orthogonalize.1 = (bf16[1024,768]{1,0:T(8,128)(2,1)S(1)}, bf16[1024,768]{1,0:T(8,128)(2,1)S(1)}) custom-call(bf16[1024,768]{1,0:T(8,128)(2,1)S(1)} %reshape.29.x_ref), custom_call_target="tpu_custom_call" | custom-call | flops 6643777536 | bytes 3145728 | tf_op jit(solution)/shard_map/orthogonalize/orthogonalize/pallas_call | solution.py:240
  68.7 0.0 copy-start
  68.8 1.1 copy-done
  69.9 1.3 reshape.30
  71.2 5.1 %all-to-all-start.2 = ((bf16[32,8,4,768]{3,2,1,0:T(4,128)(2,1)}), bf16[32,8,4,768]{3,2,1,0:T(4,128)(2,1)S(1)}, u32[]{:S(2)}, u32[]{:S(2)}) async-start(bf16[32,8,4,768]{3,2,1,0:T(4,128)(2,1)} %reshape.30), calls=%async_computation.2 | async-start | bytes 3145728 | tf_op jit(solution)/shard_map/return_dp/all_to_all | solution.py:406
  76.4 1.2 dynamic-slice_bitcast_fusion.6
  77.5 0.7 collective-permute-start.1
  78.2 4.4 %collective-permute-start = (bf16[32,4,768]{2,1,0:T(4,128)(2,1)S(1)}, bf16[32,4,768]{2,1,0:T(4,128)(2,1)S(1)}, u32[]{:S(2)}, u32[]{:S(2)}) collective-permute-start(bf16[32,4,768]{2,1,0:T(4,128)(2,1)S(1)} %get-tuple-element.66), channel_id=1, source_target_pairs={{0,3},{1,4},{2,5},{3,6},{4,7},{5,0},{6,1},{7,2},{8,11},{9,12},{10,... | collective-permute-start | bytes 589832 | tf_op jit(solution)/shard_map/return_owner_early/ppermute | solution.py:387
  82.6 13.3 %collective-permute-done.1.refs_1_ = bf16[32,4,768]{2,1,0:T(4,128)(2,1)S(1)} collective-permute-done((bf16[32,4,768]{2,1,0:T(4,128)(2,1)S(1)}, bf16[32,4,768]{2,1,0:T(4,128)(2,1)S(1)}, u32[]{:S(2)}, u32[]{:S(2)}) %collective-permute-start.1) | collective-permute-done | bytes 196640 | tf_op jit(solution)/shard_map/return_owner_early/ppermute | solution.py:387
  96.0 0.0 collective-permute-done.refs_0_
  96.0 0.6 all-to-all-done.2.parts_ref
  96.5 2.5 %pack.1 = bf16[32,10,4,768]{3,2,1,0:T(4,128)(2,1)} custom-call(s32[8,256]{1,0:T(8,128)S(1)} %get-tuple-element.42.table_ref, bf16[32,8,4,768]{3,2,1,0:T(4,128)(2,1)S(1)} %all-to-all-done.2.parts_ref, bf16[32,4,768]{2,1,0:T(4,128)(2,1)S(1)} %collective-permute-done.refs_0_, bf16[32,4,768]{2,1,0:T(4,128)(2,1)S(1)} %collective-permute-done.1.refs_1_), custom_call_target="tpu_custom_call" | custom-call | tf_op jit(solution)/shard_map/second_matrix/pack/pallas_call | solution.py:269
  99.0 6.9 %all-to-all-start.3 = ((bf16[32,10,4,768]{3,2,1,0:T(4,128)(2,1)}), bf16[32,10,4,768]{3,2,1,0:T(4,128)(2,1)S(1)}, u32[]{:S(2)}, u32[]{:S(2)}) async-start(bf16[32,10,4,768]{3,2,1,0:T(4,128)(2,1)} %pack.1), calls=%async_computation.3 | async-start | bytes 3932160 | tf_op jit(solution)/shard_map/second_matrix/all_to_all | solution.py:412
  106.0 1.2 dynamic-slice_bitcast_fusion
  107.2 1.0 collective-permute-start.6
  108.2 1.1 collective-permute-start.5
  109.3 2.8 %collective-permute-start.4 = (bf16[32,4,768]{2,1,0:T(4,128)(2,1)S(1)}, bf16[32,4,768]{2,1,0:T(4,128)(2,1)S(1)}, u32[]{:S(2)}, u32[]{:S(2)}) collective-permute-start(bf16[32,4,768]{2,1,0:T(4,128)(2,1)S(1)} %get-tuple-element.61), channel_id=1, source_target_pairs={{0,6},{1,7},{2,0},{3,1},{4,2},{5,3},{6,4},{7,5},{8,14},{9,15},{10,... | collective-permute-start | bytes 589832 | tf_op jit(solution)/shard_map/return_owner/ppermute | solution.py:387
  112.0 0.2 collective-permute-start.3
  112.2 3.1 %collective-permute-start.2 = (bf16[32,4,768]{2,1,0:T(4,128)(2,1)S(1)}, bf16[32,4,768]{2,1,0:T(4,128)(2,1)S(1)}, u32[]{:S(2)}, u32[]{:S(2)}) collective-permute-start(bf16[32,4,768]{2,1,0:T(4,128)(2,1)S(1)} %get-tuple-element.63), channel_id=1, source_target_pairs={{0,4},{1,5},{2,6},{3,7},{4,0},{5,1},{6,2},{7,3},{8,12},{9,13},{10,... | collective-permute-start | bytes 589832 | tf_op jit(solution)/shard_map/return_owner/ppermute | solution.py:387
  115.3 0.5 slice.13
  116.4 0.8 collective-permute-done.6.refs_5_
  117.3 0.0 copy-start.2
  117.3 1.2 collective-permute-done.5.refs_4_
  118.5 0.0 copy-start.4
  118.5 3.1 %collective-permute-done.4.refs_3_ = bf16[32,4,768]{2,1,0:T(4,128)(2,1)S(1)} collective-permute-done((bf16[32,4,768]{2,1,0:T(4,128)(2,1)S(1)}, bf16[32,4,768]{2,1,0:T(4,128)(2,1)S(1)}, u32[]{:S(2)}, u32[]{:S(2)}) %collective-permute-start.4) | collective-permute-done | bytes 196640 | tf_op jit(solution)/shard_map/return_owner/ppermute | solution.py:387
  121.5 0.0 copy-start.6
  121.5 12.0 %collective-permute-done.3.refs_2_ = bf16[32,4,768]{2,1,0:T(4,128)(2,1)S(1)} collective-permute-done((bf16[32,4,768]{2,1,0:T(4,128)(2,1)S(1)}, bf16[32,4,768]{2,1,0:T(4,128)(2,1)S(1)}, u32[]{:S(2)}, u32[]{:S(2)}) %collective-permute-start.3) | collective-permute-done | bytes 196640 | tf_op jit(solution)/shard_map/return_owner/ppermute | solution.py:387
  133.5 0.0 copy-start.7
  133.5 0.7 collective-permute-done.2.refs_1_
  134.2 0.0 copy-start.8
  134.2 0.0 all-to-all-done.3.early_ref
  134.2 0.0 copy-done.2
  134.2 0.0 copy-done.4
  134.2 0.0 copy-done.6
  134.2 0.0 copy-done.7
  134.2 0.6 copy-done.8
  134.9 0.0 copy-start.1
  134.9 5.7 %conditional.1 = (bf16[1024,768]{1,0:T(8,128)(2,1)}) conditional(s32[]{:T(128)} %bitcast.3, bf16[32,10,4,768]{3,2,1,0:T(4,128)(2,1)S(1)} %all-to-all-done.3.early_ref, (bf16[32,10,4,768]{3,2,1,0:T(4,128)(2,1)S(1)}, bf16[32,4,768]{2,1,0:T(4,128)(2,1)}, bf16[32,4,768]{2,1,0:T(4,128)(2,1)}, bf16[32,4,768]{2,1,0:T(4,128)(2,1)}, ...), branch_computations={%region_0.1_spmd, %region_1.2_spmd} | conditional | bytes 11010112 | solution.py:422
  134.9 2.0 %slice.9 = bf16[32,8,4,768]{3,2,1,0:T(4,128)(2,1)} slice(bf16[32,10,4,768]{3,2,1,0:T(4,128)(2,1)S(1)} %param), slice={[0:32], [0:8], [0:4], [0:768]} | slice | bytes 3145728 | tf_op jit(solution)/shard_map/second_matrix/slice | solution.py:413
  136.8 3.7 %reshape.23 = bf16[1024,768]{1,0:T(8,128)(2,1)} reshape(bf16[32,8,4,768]{3,2,1,0:T(4,128)(2,1)} %slice.9) | data formatting | bytes 3145728 | tf_op jit(solution)/shard_map/second_matrix/reshape | solution.py:413
  140.6 0.0 copy-done.1
  140.6 4.9 %finish.1 = (f32[192,4,768]{2,1,0:T(4,128)}, bf16[2,1024,768]{2,1,0:T(8,128)(2,1)}) custom-call(s32[8,256]{1,0:T(8,128)S(1)} %get-tuple-element.42.table_ref, bf16[1024,768]{1,0:T(8,128)(2,1)S(1)} %copy-done.1, bf16[1024,768]{1,0:T(8,128)(2,1)} %get-tuple-element.67.second_ref, bf16[32,10,4,768]{3,2,1,0:T(4,128)(2,1)S(1)} %all-to-all-done.3.early_ref, ...), custom_call_target="tpu_custom_call" | custom-call | tf_op jit(solution)/shard_map/finish/finish/pallas_call | solution.py:335
Async XLA Ops:
  68.7 1.1 copy-start
  71.2 25.3 %all-to-all-start.2 = ((bf16[32,8,4,768]{3,2,1,0:T(4,128)(2,1)}), bf16[32,8,4,768]{3,2,1,0:T(4,128)(2,1)S(1)}, u32[]{:S(2)}, u32[]{:S(2)}) async-start(bf16[32,8,4,768]{3,2,1,0:T(4,128)(2,1)} %reshape.30), calls=%async_computation.2 | async-start | bytes 3145728 | tf_op jit(solution)/shard_map/return_dp/all_to_all | solution.py:406
  77.5 18.4 %collective-permute-start.1 = (bf16[32,4,768]{2,1,0:T(4,128)(2,1)S(1)}, bf16[32,4,768]{2,1,0:T(4,128)(2,1)S(1)}, u32[]{:S(2)}, u32[]{:S(2)}) collective-permute-start(bf16[32,4,768]{2,1,0:T(4,128)(2,1)S(1)} %get-tuple-element.65), channel_id=1, source_target_pairs={{0,5},{1,6},{2,7},{3,0},{4,1},{5,2},{6,3},{7,4},{8,13},{9,14},{10,... | collective-permute-start | bytes 589832 | tf_op jit(solution)/shard_map/return_owner_early/ppermute | solution.py:387
  78.2 17.7 %collective-permute-start = (bf16[32,4,768]{2,1,0:T(4,128)(2,1)S(1)}, bf16[32,4,768]{2,1,0:T(4,128)(2,1)S(1)}, u32[]{:S(2)}, u32[]{:S(2)}) collective-permute-start(bf16[32,4,768]{2,1,0:T(4,128)(2,1)S(1)} %get-tuple-element.66), channel_id=1, source_target_pairs={{0,3},{1,4},{2,5},{3,6},{4,7},{5,0},{6,1},{7,2},{8,11},{9,12},{10,... | collective-permute-start | bytes 589832 | tf_op jit(solution)/shard_map/return_owner_early/ppermute | solution.py:387
  99.0 35.1 %all-to-all-start.3 = ((bf16[32,10,4,768]{3,2,1,0:T(4,128)(2,1)}), bf16[32,10,4,768]{3,2,1,0:T(4,128)(2,1)S(1)}, u32[]{:S(2)}, u32[]{:S(2)}) async-start(bf16[32,10,4,768]{3,2,1,0:T(4,128)(2,1)} %pack.1), calls=%async_computation.3 | async-start | bytes 3932160 | tf_op jit(solution)/shard_map/second_matrix/all_to_all | solution.py:412
  107.2 10.0 %collective-permute-start.6 = (bf16[32,4,768]{2,1,0:T(4,128)(2,1)S(1)}, bf16[32,4,768]{2,1,0:T(4,128)(2,1)S(1)}, u32[]{:S(2)}, u32[]{:S(2)}) collective-permute-start(bf16[32,4,768]{2,1,0:T(4,128)(2,1)S(1)} %get-tuple-element.59), channel_id=1, source_target_pairs={{0,7},{1,0},{2,1},{3,2},{4,3},{5,4},{6,5},{7,6},{8,15},{9,8},{10,9... | collective-permute-start | bytes 589832 | tf_op jit(solution)/shard_map/return_owner/ppermute | solution.py:387
  108.2 10.3 %collective-permute-start.5 = (bf16[32,4,768]{2,1,0:T(4,128)(2,1)S(1)}, bf16[32,4,768]{2,1,0:T(4,128)(2,1)S(1)}, u32[]{:S(2)}, u32[]{:S(2)}) collective-permute-start(bf16[32,4,768]{2,1,0:T(4,128)(2,1)S(1)} %get-tuple-element.60), channel_id=1, source_target_pairs={{0,1},{1,2},{2,3},{3,4},{4,5},{5,6},{6,7},{7,0},{8,9},{9,10},{10,1... | collective-permute-start | bytes 589832 | tf_op jit(solution)/shard_map/return_owner/ppermute | solution.py:387
  109.3 12.3 %collective-permute-start.4 = (bf16[32,4,768]{2,1,0:T(4,128)(2,1)S(1)}, bf16[32,4,768]{2,1,0:T(4,128)(2,1)S(1)}, u32[]{:S(2)}, u32[]{:S(2)}) collective-permute-start(bf16[32,4,768]{2,1,0:T(4,128)(2,1)S(1)} %get-tuple-element.61), channel_id=1, source_target_pairs={{0,6},{1,7},{2,0},{3,1},{4,2},{5,3},{6,4},{7,5},{8,14},{9,15},{10,... | collective-permute-start | bytes 589832 | tf_op jit(solution)/shard_map/return_owner/ppermute | solution.py:387
  112.0 21.5 %collective-permute-start.3 = (bf16[32,4,768]{2,1,0:T(4,128)(2,1)S(1)}, bf16[32,4,768]{2,1,0:T(4,128)(2,1)S(1)}, u32[]{:S(2)}, u32[]{:S(2)}) collective-permute-start(bf16[32,4,768]{2,1,0:T(4,128)(2,1)S(1)} %get-tuple-element.62), channel_id=1, source_target_pairs={{0,2},{1,3},{2,4},{3,5},{4,6},{5,7},{6,0},{7,1},{8,10},{9,11},{10,... | collective-permute-start | bytes 589832 | tf_op jit(solution)/shard_map/return_owner/ppermute | solution.py:387
  112.2 22.0 %collective-permute-start.2 = (bf16[32,4,768]{2,1,0:T(4,128)(2,1)S(1)}, bf16[32,4,768]{2,1,0:T(4,128)(2,1)S(1)}, u32[]{:S(2)}, u32[]{:S(2)}) collective-permute-start(bf16[32,4,768]{2,1,0:T(4,128)(2,1)S(1)} %get-tuple-element.63), channel_id=1, source_target_pairs={{0,4},{1,5},{2,6},{3,7},{4,0},{5,1},{6,2},{7,3},{8,12},{9,13},{10,... | collective-permute-start | bytes 589832 | tf_op jit(solution)/shard_map/return_owner/ppermute | solution.py:387
  117.3 16.9 %copy-start.2 = (bf16[32,4,768]{2,1,0:T(4,128)(2,1)}, bf16[32,4,768]{2,1,0:T(4,128)(2,1)S(1)}, u32[]{:S(2)}) copy-start(bf16[32,4,768]{2,1,0:T(4,128)(2,1)S(1)} %collective-permute-done.6.refs_5_) | copy-start | bytes 589828
  118.5 15.7 %copy-start.4 = (bf16[32,4,768]{2,1,0:T(4,128)(2,1)}, bf16[32,4,768]{2,1,0:T(4,128)(2,1)S(1)}, u32[]{:S(2)}) copy-start(bf16[32,4,768]{2,1,0:T(4,128)(2,1)S(1)} %collective-permute-done.5.refs_4_) | copy-start | bytes 589828
  121.5 12.7 %copy-start.6 = (bf16[32,4,768]{2,1,0:T(4,128)(2,1)}, bf16[32,4,768]{2,1,0:T(4,128)(2,1)S(1)}, u32[]{:S(2)}) copy-start(bf16[32,4,768]{2,1,0:T(4,128)(2,1)S(1)} %collective-permute-done.4.refs_3_) | copy-start | bytes 589828
  133.5 0.7 copy-start.7
  134.2 0.7 copy-start.8
  134.9 5.7 %copy-start.1 = (bf16[1024,768]{1,0:T(8,128)(2,1)S(1)}, bf16[1024,768]{1,0:T(8,128)(2,1)}, u32[]{:S(2)}) copy-start(bf16[1024,768]{1,0:T(8,128)(2,1)} %copy-done) | copy-start | bytes 4718596

commit v3 on v2

--- a/solution.py
+++ b/solution.py
@@ -17,7 +17,7 @@
 quintic_three = 2.0315
 norm_epsilon = 1e-07
 
-SLOT, FIRST, SECOND, SPILLED, PART, MATRIX, HELPER_INDEX = range(7)
+SLOT, FIRST, SECOND, SPILLED, PART, MATRIX, HELPER_INDEX, HELPER = range(8)
 TABLE_ROWS = 8
 
 
@@ -68,17 +68,30 @@
     second_index = total(before_row & plane & (second_col == 1.0), 0)
     pair = plane & (first_col == 0.0) & (second_row == 1.0) & (free_index == second_index)
     left_row = second_row - total(pair, 0)
-    idle_col = 1.0 - first_col - total(pair, 1)
-    left_col = column(left_row)
-    idle_row = jnp.sum(jnp.where(up == down, idle_col, 0.0), axis=0, keepdims=True)
-    left_index = total(before_row & (left_col == 1.0), 0)
-    idle_index = total(before_col & (idle_row == 1.0), 1)
-    spill = (left_row == 1.0) & (idle_col == 1.0) & (left_index == idle_index)
-    helper_row = jnp.sum(jnp.where(pair | spill, up.astype(f32), 0.0), axis=0, keepdims=True)
+    spilled = jnp.sum(left_row, axis=1, keepdims=True)
+
+    def put(row, values):
+        table_ref[row : row + 1, : values.shape[1]] = values.astype(jnp.int32)
+
+    def helpers(pairs):
+        return jnp.sum(jnp.where(pairs, up.astype(f32), 0.0), axis=0, keepdims=True)
+
+    table_ref[...] = jnp.zeros_like(table_ref)
+    put(HELPER, helpers(pair))
+
+    @pl.when(jnp.sum(left_row) > 0.0)
+    def _():
+        idle_col = 1.0 - first_col - total(pair, 1)
+        left_col = column(left_row)
+        idle_row = jnp.sum(jnp.where(up == down, idle_col, 0.0), axis=0, keepdims=True)
+        left_index = total(before_row & (left_col == 1.0), 0)
+        idle_index = total(before_col & (idle_row == 1.0), 1)
+        put(HELPER, helpers(pair | ((left_row == 1.0) & (idle_col == 1.0) & (left_index == idle_index))))
+
+    helper_row = table_ref[HELPER : HELPER + 1, :].astype(f32)
     helper_col = column(helper_row)
     helper_of = jnp.sum(jnp.where(held, helper_col, 0.0), axis=0, keepdims=True)
     slot_row = jnp.where(rank_row == 0.0, own_row, helper_of)
-    spilled = jnp.sum(left_row, axis=1, keepdims=True)
     slot_row = slot_row.astype(jnp.int32)
     helper_row = helper_row.astype(jnp.int32)
     shift = planes.bit_length() - 1
@@ -99,10 +112,6 @@
     helper_here = column(helper_row.astype(f32))
     part_row = jnp.sum(jnp.where(mine, helper_here, 0.0), axis=0, keepdims=True).astype(jnp.int32) >> shift
 
-    def put(row, values):
-        table_ref[row : row + 1, : values.shape[1]] = values.astype(jnp.int32)
-
-    table_ref[...] = jnp.zeros_like(table_ref)
     put(SLOT, slot_row)
     put(FIRST, first_row)
     put(SECOND, second_row)
@@ -190,11 +199,14 @@
     )(owner_table.reshape(1, mats), momentum, grad)
 
 
-def orthogonalize_kernel(scale, x_ref, out_ref, again_ref, iterate_ref, gram_ref, poly_ref):
+def orthogonalize_kernel(scale, x_ref, out_ref, again_ref, iterate_ref, gram_ref, poly_ref, sem):
     rows, cols = x_ref.shape
     tile, side = min(256, rows), min(256, cols) if cols % 256 == 0 else 128
     f32, bf16 = jnp.float32, jnp.bfloat16
     starts = range(0, cols, side)
+
+    def copy_out(i):
+        return pltpu.make_async_copy(again_ref.at[pl.ds(i, tile)], out_ref.at[pl.ds(i, tile)], sem.at[i // tile])
 
     def put(ref, i, block):
         ref[i : i + side, i:] = block
@@ -217,7 +229,7 @@
             step = step * jnp.asarray(scale, bf16) if last else step
             target_ref[i : i + tile, :] = step
             if last:
-                again_ref[i : i + tile, :] = step
+                copy_out(i).start()
 
     gram = [gram_rows(x_ref, i) for i in starts]
     diagonal = lax.broadcasted_iota(jnp.int32, (side, side), 0) == lax.broadcasted_iota(jnp.int32, (side, side), 1)
@@ -232,7 +244,9 @@
         for i in starts:
             put(gram_ref, i, gram_rows(iterate_ref, i).astype(bf16))
         poly()
-        apply(iterate_ref, out_ref, None, True)
+        apply(iterate_ref, again_ref, None, True)
+    for i in range(0, rows, tile):
+        copy_out(i).wait()
 
 
 def orthogonalize(matrix, scale):
@@ -240,10 +254,12 @@
     return pl.pallas_call(
         functools.partial(orthogonalize_kernel, scale),
         out_shape=[jax.ShapeDtypeStruct((rows, cols), jnp.bfloat16)] * 2,
+        out_specs=[pl.BlockSpec(memory_space=pltpu.HBM), pl.BlockSpec(memory_space=pltpu.VMEM)],
         scratch_shapes=[
             pltpu.VMEM((rows, cols), jnp.bfloat16),
             pltpu.VMEM((cols, cols), jnp.bfloat16),
             pltpu.VMEM((cols, cols), jnp.bfloat16),
+            pltpu.SemaphoreType.DMA((rows // min(256, rows),)),
         ],
         compiler_params=pltpu.CompilerParams(vmem_limit_bytes=24 * 1024 * 1024),
         cost_estimate=pl.CostEstimate(flops=ITERS * 2 * cols * cols * (2 * rows + cols), bytes_accessed=4 * rows * cols, transcendentals=0),
@@ -251,113 +267,144 @@
     )(matrix)
 
 
-def pack_kernel(table_ref, parts_ref, *refs):
-    early_refs, out_ref = refs[:-1], refs[-1]
-    block = out_ref.shape[0]
-    groups = parts_ref.shape[1]
-    first = pl.program_id(0) * block
-    for k, early_ref in enumerate(early_refs):
-        out_ref[:, groups + k] = early_ref[...]
-    for i in range(block):
-        out_ref[i, :groups] = parts_ref[table_ref[PART, first + i]]
-
-
-def pack(table, parts, early, steps=4):
-    count, groups, rows, cols = parts.shape
-    block = count // steps
-    shape = (count, groups + len(early), rows, cols)
+def pack_kernel(table_ref, parts_ref, early_ref, out_ref, sem):
+    count, rows, _ = parts_ref.shape
+    copies = [pltpu.make_async_copy(early_ref, out_ref.at[:, pl.ds(rows, early_ref.shape[1])], sem.at[count])]
+    for i in range(count):
+        to_ref = out_ref.at[i, pl.ds(0, rows)]
+        copies.append(pltpu.make_async_copy(parts_ref.at[table_ref[PART, i]], to_ref, sem.at[i]))
+    for copy in copies:
+        copy.start()
+    for copy in copies:
+        copy.wait()
+
+
+def pack(table, parts, early):
+    count, rows, cols = parts.shape
     return pl.pallas_call(
         pack_kernel,
         grid_spec=pltpu.PrefetchScalarGridSpec(
             num_scalar_prefetch=1,
-            grid=(steps,),
-            in_specs=[
-                pl.BlockSpec(parts.shape, lambda i, *_: (0, 0, 0, 0)),
-                *(pl.BlockSpec((block, rows, cols), lambda i, *_: (i, 0, 0)) for _ in early),
-            ],
-            out_specs=pl.BlockSpec((block, *shape[1:]), lambda i, *_: (i, 0, 0, 0)),
+            grid=(1,),
+            in_specs=[pl.BlockSpec(x.shape, lambda *_: (0, 0, 0)) for x in (parts, early)],
+            out_specs=pl.BlockSpec(memory_space=pltpu.HBM),
+            scratch_shapes=[pltpu.SemaphoreType.DMA((count + 1,))],
         ),
-        out_shape=jax.ShapeDtypeStruct(shape, parts.dtype),
+        out_shape=jax.ShapeDtypeStruct((count, rows + early.shape[1], cols), parts.dtype),
         compiler_params=pltpu.CompilerParams(vmem_limit_bytes=14 * 1024 * 1024),
         name="pack",
-    )(table, parts, *early)
-
-
-def finish_kernel(late, table_ref, mine_ref, second_ref, early_ref, *refs):
-    late_refs, (update_ref, owned_ref, staged_ref, zero_ref, sem, owned_sem) = refs[:late], refs[late:]
+    )(table, parts, early)
+
+
+def put_owned(table_ref, slot, copies, owned_ref, zero_ref, sem, act):
     me = lax.axis_index("dp") * lax.axis_size("owner") + lax.axis_index("owner")
     tile = zero_ref.shape[0]
+    present = table_ref[FIRST + slot, me] > 0
+
+    @pl.when(present)
+    def _():
+        for copy in copies:
+            act(copy)
+
+    @pl.when(jnp.logical_not(present))
+    def _():
+        for i in range(owned_ref.shape[1] // tile):
+            act(pltpu.make_async_copy(zero_ref, owned_ref.at[slot, pl.ds(i * tile, tile)], sem.at[i]))
+
+
+def put_rows(table_ref, position, rows, staged_ref, update_ref, sem):
+    count = rows.shape[0]
+    staged_ref[...] = rows.astype(jnp.float32)
+
+    def each(i, _):
+        matrix = table_ref[MATRIX, position + i]
+
+        @pl.when(matrix >= 0)
+        def _():
+            pltpu.make_async_copy(staged_ref.at[i], update_ref.at[matrix], sem).start()
+
+    lax.fori_loop(0, count, each, None, unroll=8 if count % 8 == 0 else 1)
+
+
+def begin_kernel(table_ref, mine_ref, owned_ref, zero_ref, sem):
     zero_ref[...] = jnp.zeros_like(zero_ref)
-
-    def owned(act):
-        for slot, source_ref in enumerate((mine_ref, second_ref)):
-            present = table_ref[FIRST + slot, me] > 0
-
-            @pl.when(present)
-            def _():
-                act(pltpu.make_async_copy(source_ref, owned_ref.at[slot], owned_sem.at[slot, 0]))
-
-            @pl.when(jnp.logical_not(present))
-            def _():
-                for i in range(source_ref.shape[0] // tile):
-                    to_ref = owned_ref.at[slot, pl.ds(i * tile, tile)]
-                    act(pltpu.make_async_copy(zero_ref, to_ref, owned_sem.at[slot, i]))
-
-    owned(lambda copy: copy.start())
-    count = early_ref.shape[0]
+    copy = pltpu.make_async_copy(mine_ref, owned_ref.at[0], sem.at[0])
+    put_owned(table_ref, 0, [copy], owned_ref, zero_ref, sem, lambda copy: copy.start())
+    put_owned(table_ref, 0, [copy], owned_ref, zero_ref, sem, lambda copy: copy.wait())
+
+
+def begin(table, mine):
+    hbm = pl.BlockSpec(memory_space=pltpu.HBM)
+    rows, cols = mine.shape
+    tile = min(256, rows)
+    return pl.pallas_call(
+        begin_kernel,
+        grid_spec=pltpu.PrefetchScalarGridSpec(
+            num_scalar_prefetch=1,
+            grid=(1,),
+            in_specs=[pl.BlockSpec((rows, cols), lambda *_: (0, 0))],
+            out_specs=hbm,
+            scratch_shapes=[pltpu.VMEM((tile, cols), mine.dtype), pltpu.SemaphoreType.DMA((rows // tile,))],
+        ),
+        out_shape=jax.ShapeDtypeStruct((CAP, rows, cols), mine.dtype),
+        compiler_params=pltpu.CompilerParams(vmem_limit_bytes=8 * 1024 * 1024),
+        cost_estimate=pl.CostEstimate(flops=0, bytes_accessed=4 * rows * cols, transcendentals=0),
+        name="begin",
+    )(table, mine)
+
+
+def finish_kernel(late, table_ref, packed_ref, *refs):
+    late_refs, refs = refs[:late], refs[late + 1 :]
+    update_ref, owned_ref, staged_ref, zero_ref, sem, owned_sem = refs
+    zero_ref[...] = jnp.zeros_like(zero_ref)
+    count, rows, _ = late_refs[0].shape
+    keep = owned_ref.shape[1] // count
+    copies = [
+        pltpu.make_async_copy(packed_ref.at[i, pl.ds(0, keep)], owned_ref.at[1, pl.ds(i * keep, keep)], owned_sem.at[i])
+        for i in range(count)
+    ]
+    put_owned(table_ref, 1, copies, owned_ref, zero_ref, owned_sem, lambda copy: copy.start())
+    early_rows = packed_ref[:, keep:, :].astype(jnp.float32)
     pieces = [lambda ref=ref: ref[...] for ref in late_refs]
-    pieces += [lambda k=k: early_ref[:, k] for k in range(early_ref.shape[1])]
+    pieces += [lambda i=i: early_rows[:, i : i + rows, :] for i in range(0, early_rows.shape[1], rows)]
     for k, piece in enumerate(pieces):
-        staged_ref[k * count : (k + 1) * count] = piece().astype(jnp.float32)
-
-        def each(i, _, at=k * count):
-            matrix = table_ref[MATRIX, at + i]
-
-            @pl.when(matrix >= 0)
-            def _():
-                pltpu.make_async_copy(staged_ref.at[at + i], update_ref.at[matrix], sem).start()
-
-        lax.fori_loop(0, count, each, None, unroll=8 if count % 8 == 0 else 1)
+        put_rows(table_ref, k * count, piece(), staged_ref.at[pl.ds(k * count, count)], update_ref, sem)
+    put_owned(table_ref, 1, copies, owned_ref, zero_ref, owned_sem, lambda copy: copy.wait())
+
     pltpu.make_async_copy(staged_ref.at[pl.ds(0, update_ref.shape[0])], update_ref, sem).wait()
-    owned(lambda copy: copy.wait())
-
-
-def finish(table, late, mine, second, packed, mats):
+
+
+def finish(table, late, packed, owned, mats):
     count, rows, cols = late[0].shape
-    groups, early = packed.shape[1], packed.shape[1] - second.shape[0] // (count * rows)
+    early = packed.shape[1] // rows - owned.shape[1] // (count * rows)
     hbm = pl.BlockSpec(memory_space=pltpu.HBM)
-    tile = min(256, mine.shape[0])
+    tile = min(256, owned.shape[1])
 
     def whole(x):
         return pl.BlockSpec(x.shape, lambda *_: (0,) * len(x.shape))
 
-    owned_shape = (CAP, *mine.shape)
     return pl.pallas_call(
         functools.partial(finish_kernel, len(late)),
         grid_spec=pltpu.PrefetchScalarGridSpec(
             num_scalar_prefetch=1,
             grid=(1,),
-            in_specs=[
-                whole(mine),
-                whole(second),
-                pl.BlockSpec((count, early, rows, cols), lambda *_: (0, groups // early - 1, 0, 0)),
-                *(whole(piece) for piece in late),
-            ],
+            in_specs=[whole(packed), *(whole(piece) for piece in late), hbm],
             out_specs=[hbm, hbm],
             scratch_shapes=[
                 pltpu.VMEM(((len(late) + early) * count, rows, cols), jnp.float32),
-                pltpu.VMEM((tile, cols), mine.dtype),
+                pltpu.VMEM((tile, cols), owned.dtype),
                 pltpu.SemaphoreType.DMA,
-                pltpu.SemaphoreType.DMA((CAP, mine.shape[0] // tile)),
+                pltpu.SemaphoreType.DMA((max(count, owned.shape[1] // tile),)),
             ],
         ),
         out_shape=[
             jax.ShapeDtypeStruct((mats, rows, cols), jnp.float32),
-            jax.ShapeDtypeStruct(owned_shape, mine.dtype),
+            jax.ShapeDtypeStruct(owned.shape, owned.dtype),
         ],
+        input_output_aliases={2 + len(late): 1},
         compiler_params=pltpu.CompilerParams(vmem_limit_bytes=24 * 1024 * 1024),
         name="finish",
-    )(table, mine, second, packed, *late)
+    )(table, packed, *late, owned)
 
 
 def spilled_kernel(table_ref, arrived_ref, out_ref):
@@ -378,14 +425,18 @@
     )(table, arrived)
 
 
-def send_planes(rows, way):
+def to_planes(rows, way):
+    me, planes = lax.axis_index("owner"), lax.axis_size("owner")
+    count = rows.shape[1] // planes
+    return [lax.dynamic_slice_in_dim(rows, lax.rem(me + far, planes) * count, count, 1) for far in way]
+
+
+def send(pieces, way):
     planes = lax.axis_size("owner")
-    me = lax.axis_index("owner")
-    arrived = []
-    for far in way:
-        piece = lax.dynamic_index_in_dim(rows, lax.rem(me + far, planes), 1, keepdims=False)
-        arrived.append(lax.ppermute(piece, "owner", [(i, (i + far) % planes) for i in range(planes)]) if far else piece)
-    return arrived
+    return [
+        lax.ppermute(piece, "owner", [(i, (i + far) % planes) for i in range(planes)]) if far else piece
+        for piece, far in zip(pieces, way)
+    ]
 
 
 def shards(momentum, grad, owner_table):
@@ -394,6 +445,7 @@
     devices = dp_count * planes
     mats, rows, cols = momentum.shape
     whole_rows = devices * rows
+
     with jax.named_scope("start"):
         table, new_momentum, outgoing = start(owner_table, momentum, grad, planes, devices)
     with jax.named_scope("gather_matrix"):
@@ -402,26 +454,29 @@
     with jax.named_scope("orthogonalize"):
         mine, again = orthogonalize(matrix, math.sqrt(whole_rows))
     with jax.named_scope("return_dp"):
-        groups = again.reshape(dp_count, planes, rows, cols)
-        parts = lax.all_to_all(groups, "dp", 0, 0, tiled=True)
+        parts = lax.all_to_all(mine.reshape(dp_count, planes * rows, cols), "dp", 0, 0, tiled=True)
     with jax.named_scope("return_owner_early"):
-        early = send_planes(groups, early_distances(planes))
+        way = early_distances(planes)
+        early = jnp.concatenate(send(to_planes(again.reshape(dp_count, planes * rows, cols), way), way), 1)
     with jax.named_scope("return_owner"):
-        late = send_planes(parts, [0, *late_distances(planes)])
+        way = [0, *late_distances(planes)]
+        late = send(to_planes(parts, way), way)
     with jax.named_scope("second_matrix"):
         packed = lax.all_to_all(pack(table, parts, early), "dp", 0, 0, tiled=True)
-        second = packed[:, :planes].reshape(whole_rows, cols)
-
-    def with_spilled(second, packed, *late):
-        arrived = jnp.concatenate([*late, *(packed[:, planes + i] for i in range(len(early)))])
+
+    with jax.named_scope("begin"):
+        owned = begin(table, mine)
+
+    def with_spilled(packed, *late):
+        came_early = packed[:, planes * rows :].reshape(dp_count, -1, rows, cols)
+        arrived = jnp.concatenate([*late, *(came_early[:, i] for i in range(came_early.shape[1]))])
         rows_out = lax.all_to_all(spilled_rows(table, arrived), ("dp", "owner"), 0, 0, tiled=True)
-        return rows_out.reshape(whole_rows, cols)
+        return jnp.concatenate([rows_out.reshape(dp_count, planes * rows, cols), packed[:, planes * rows :]], 1)
 
     with jax.named_scope("spilled"):
-        spilled = table[SPILLED, 0] > 0
-        second = lax.cond(spilled, with_spilled, lambda second, *_: second, second, packed, *late)
+        packed = lax.cond(table[SPILLED, 0] > 0, with_spilled, lambda packed, *late: packed, packed, *late)
     with jax.named_scope("finish"):
-        update, owned = finish(table, late, mine, second, packed, mats)
+        update, owned = finish(table, late, packed, owned, mats)
     return new_momentum, update, owned[:, None]
 
 

time: 146 us -> 138 us (0.945)
  local copies, waits for them, and re-layouts: 12.1 us -> 3.12 us
  waiting for transfers between devices: 31.7 us -> 27.8 us
  Pallas kernels: 18.6 us -> 21.6 us
    ppermute x7, waiting for transfers between devices: 31.1 us -> 24.4 us  [send(): lax.ppermute(piece, 'owner', [(i, (i + far) % planes) for i in range(plan...]
    reshape x2 -> x0, local copies, waits for them, and re-layouts: 5.04 us -> none  [the longest x1 3.72 us: shards(): second = packed[:, :planes].reshape(whole_rows, cols)]
    pallas_call x0 -> x1, Pallas kernels: none -> 3.27 us  [begin(): pl.pallas_call(begin_kernel, grid_spec=pltpu.PrefetchScalarGridSpec(num_s...]
    all_to_all x1, waiting for transfers between devices: 0.56 us -> 3.41 us  [shards(): lax.all_to_all(mine.reshape(dp_count, planes * rows, cols), 'dp', 0, 0, t...]
    squeeze x2 -> x0, local copies, waits for them, and re-layouts: 2.4 us -> none  [send_planes(): lax.dynamic_index_in_dim(rows, lax.rem(me + far, planes), 1, keepdims=False)]
    slice x2 -> x1, local copies, waits for them, and re-layouts: 2.49 us -> 0.51 us  [shards(): table[SPILLED, 0] > 0]
    dynamic_slice x0 -> x2, local copies, waits for them, and re-layouts: none -> 1.55 us  [to_planes(): lax.dynamic_slice_in_dim(rows, lax.rem(me + far, planes) * count, count, 1)]
  transfers between devices with their start and end apart: 9 -> 9, of which waited for: 7 -> 3; matrix products, arithmetic and copies ran while one was open for 2% -> 2% of each run, Pallas kernels for 0% -> 2%
where the time goes in v3:
time: 138 us; the launch traced here: 137 us
  blocking collectives  56.5 us (41%)
  waiting for transfers between devices  27.8 us (20%)
  starting transfers between devices  26.5 us (19%)
  Pallas kernels  21.6 us (16%)
  local copies, waits for them, and re-layouts  3.12 us (2%)
  between operations  1.63 us (1%)
    all_to_all x1, blocking collectives, shards(): received = lax.all_to_all(outgoing, ('dp', 'owner'), 0, 0, tiled=True)  56.5 us
    ppermute x7, waiting for transfers between devices, send(): lax.ppermute(piece, 'owner', [(i, (i + far) % planes) for i in range(plan...  24.4 us
    ppermute x7, starting transfers between devices, send(): lax.ppermute(piece, 'owner', [(i, (i + far) % planes) for i in range(plan...  14.5 us
    all_to_all x1, starting transfers between devices, shards(): packed = lax.all_to_all(pack(table, parts, early), 'dp', 0, 0, tiled=True)  6.93 us
    pallas_call x1, Pallas kernels, orthogonalize(): pl.pallas_call(functools.partial(orthogonalize_kernel, scale), out_shape=...  6.81 us
    all_to_all x1, starting transfers between devices, shards(): lax.all_to_all(mine.reshape(dp_count, planes * rows, cols), 'dp', 0, 0, t...  5.12 us
    pallas_call x1, Pallas kernels, start(): pl.pallas_call(functools.partial(start_kernel, planes), grid_spec=pltpu.P...  5.09 us
    pallas_call x1, Pallas kernels, finish(): pl.pallas_call(functools.partial(finish_kernel, len(late)), grid_spec=plt...  4.27 us
  transfers between devices with their start and end apart: 9, of which 3 were waited for; matrix products, arithmetic and copies ran while one was open for 2% of the time, Pallas kernels for 2%

profile of v3, /device:TPU:34, one launch (start us, length us, event | category | flops | bytes accessed | tf_op | source)
XLA Modules:
  0.0 137.4 jit_solution(5980144505451998944)
XLA Ops:
  0.6 5.1 %start.1 = (s32[8,256]{1,0:T(8,128)S(1)}, f32[192,4,768]{2,1,0:T(4,128)}, bf16[256,4,768]{2,1,0:T(4,128)(2,1)}) custom-call(s32[1,192]{1,0:T(1,128)} %bitcast.19, f32[192,4,768]{2,1,0:T(4,128)} %momentum_ref.1, bf16[192,4,768]{2,1,0:T(4,128)(2,1)} %grad_ref.1), custom_call_target="tpu_custom_call" | custom-call | tf_op jit(solution)/shard_map/start/start/pallas_call | solution.py:172
  5.7 56.5 %all_to_all.22 = bf16[256,4,768]{2,1,0:T(4,128)(2,1)S(1)} all-to-all(bf16[256,4,768]{2,1,0:T(4,128)(2,1)} %get-tuple-element.40), channel_id=1, replica_groups=mesh['dp'=32,'owner'=8] {'dp','owner'}, dimensions={0} | all-to-all | bytes 3145728 | tf_op jit(solution)/shard_map/gather_matrix/all_to_all | solution.py:452
  62.2 0.4 reshape.29.x_ref
  62.6 6.8 %orthogonalize.1 = (bf16[1024,768]{1,0:T(8,128)(2,1)}, bf16[1024,768]{1,0:T(8,128)(2,1)S(1)}) custom-call(bf16[1024,768]{1,0:T(8,128)(2,1)S(1)} %reshape.29.x_ref), custom_call_target="tpu_custom_call" | custom-call | flops 6643777536 | bytes 3145728 | tf_op jit(solution)/shard_map/orthogonalize/orthogonalize/pallas_call | solution.py:254
  69.4 5.1 %all-to-all-start.2 = ((bf16[32,32,768]{2,1,0:T(8,128)(2,1)}), bf16[32,32,768]{2,1,0:T(8,128)(2,1)S(1)}, u32[]{:S(2)}, u32[]{:S(2)}) async-start(bf16[32,32,768]{2,1,0:T(8,128)(2,1)} %bitcast.5), calls=%async_computation.2 | async-start | bytes 3145728 | tf_op jit(solution)/shard_map/return_dp/all_to_all | solution.py:457
  74.6 0.2 constant_dynamic-slice_fusion.7
  74.8 0.6 collective-permute-start
  75.5 4.5 %collective-permute-start.1 = (bf16[32,4,768]{2,1,0:T(4,128)(2,1)S(1)}, bf16[32,4,768]{2,1,0:T(4,128)(2,1)S(1)}, u32[]{:S(2)}, u32[]{:S(2)}) collective-permute-start(bf16[32,4,768]{2,1,0:T(4,128)(2,1)S(1)} %get-tuple-element.68), channel_id=1, source_target_pairs={{0,5},{1,6},{2,7},{3,0},{4,1},{5,2},{6,3},{7,4},{8,13},{9,14},{10,... | collective-permute-start | bytes 589832 | tf_op jit(solution)/shard_map/return_owner_early/ppermute | solution.py:437
  79.9 11.2 %collective-permute-done = bf16[32,4,768]{2,1,0:T(4,128)(2,1)S(1)} collective-permute-done((bf16[32,4,768]{2,1,0:T(4,128)(2,1)S(1)}, bf16[32,4,768]{2,1,0:T(4,128)(2,1)S(1)}, u32[]{:S(2)}, u32[]{:S(2)}) %collective-permute-start) | collective-permute-done | bytes 196640 | tf_op jit(solution)/shard_map/return_owner_early/ppermute | solution.py:437
  91.2 0.0 collective-permute-done.1
  91.2 0.2 pad_maximum_fusion.1.early_ref
  91.4 3.4 %all-to-all-done.2.parts_ref = bf16[32,32,768]{2,1,0:T(8,128)(2,1)S(1)} async-done(((bf16[32,32,768]{2,1,0:T(8,128)(2,1)}), bf16[32,32,768]{2,1,0:T(8,128)(2,1)S(1)}, u32[]{:S(2)}, u32[]{:S(2)}) %all-to-all-start.2) | async-done | bytes 1572896 | tf_op jit(solution)/shard_map/return_dp/all_to_all | solution.py:457
  94.8 2.2 %pack.1 = bf16[32,40,768]{2,1,0:T(8,128)(2,1)} custom-call(s32[8,256]{1,0:T(8,128)S(1)} %get-tuple-element.39.table_ref, bf16[32,32,768]{2,1,0:T(8,128)(2,1)S(1)} %all-to-all-done.2.parts_ref, bf16[32,8,768]{2,1,0:T(8,128)(2,1)S(1)} %pad_maximum_fusion.1.early_ref), custom_call_target="tpu_custom_call" | custom-call | tf_op jit(solution)/shard_map/second_matrix/pack/pallas_call | solution.py:284
  97.0 6.9 %all-to-all-start.3 = ((bf16[32,40,768]{2,1,0:T(8,128)(2,1)}), bf16[32,40,768]{2,1,0:T(8,128)(2,1)S(1)}, u32[]{:S(2)}, u32[]{:S(2)}) async-start(bf16[32,40,768]{2,1,0:T(8,128)(2,1)} %pack.1), calls=%async_computation.3 | async-start | bytes 3932160 | tf_op jit(solution)/shard_map/second_matrix/all_to_all | solution.py:465
  103.9 1.3 constant_dynamic-slice_fusion
  105.3 1.0 collective-permute-start.6
  106.2 1.1 collective-permute-start.5
  107.3 3.5 %collective-permute-start.4 = (bf16[32,4,768]{2,1,0:T(4,128)(2,1)S(1)}, bf16[32,4,768]{2,1,0:T(4,128)(2,1)S(1)}, u32[]{:S(2)}, u32[]{:S(2)}) collective-permute-start(bf16[32,4,768]{2,1,0:T(4,128)(2,1)S(1)} %get-tuple-element.63), channel_id=1, source_target_pairs={{0,6},{1,7},{2,0},{3,1},{4,2},{5,3},{6,4},{7,5},{8,14},{9,15},{10,... | collective-permute-start | bytes 589832 | tf_op jit(solution)/shard_map/return_owner/ppermute | solution.py:437
  110.8 0.0 collective-permute-start.3
  110.8 3.9 %collective-permute-start.2 = (bf16[32,4,768]{2,1,0:T(4,128)(2,1)S(1)}, bf16[32,4,768]{2,1,0:T(4,128)(2,1)}, u32[]{:S(2)}, u32[]{:S(2)}) collective-permute-start(bf16[32,4,768]{2,1,0:T(4,128)(2,1)S(1)} %get-tuple-element.65), channel_id=1, source_target_pairs={{0,4},{1,5},{2,6},{3,7},{4,0},{5,1},{6,2},{7,3},{8,12},{9,13},{10,... | collective-permute-start | bytes 589832 | tf_op jit(solution)/shard_map/return_owner/ppermute | solution.py:437
  114.6 0.5 slice.13
  115.8 3.3 %begin.1.refs_6_ = bf16[2,1024,768]{2,1,0:T(8,128)(2,1)} custom-call(s32[8,256]{1,0:T(8,128)S(1)} %get-tuple-element.39.table_ref, bf16[1024,768]{1,0:T(8,128)(2,1)} %get-tuple-element.41.mine_ref), custom_call_target="tpu_custom_call" | custom-call | bytes 3145728 | tf_op jit(solution)/shard_map/begin/begin/pallas_call | solution.py:340
  119.1 0.0 collective-permute-done.6.refs_5_
  119.1 0.0 copy-start
  119.1 0.0 collective-permute-done.5.refs_4_
  119.1 0.0 copy-start.2
  119.1 0.0 collective-permute-done.4.refs_3_
  119.1 0.0 copy-start.4
  119.2 13.1 %collective-permute-done.3.refs_2_ = bf16[32,4,768]{2,1,0:T(4,128)(2,1)S(1)} collective-permute-done((bf16[32,4,768]{2,1,0:T(4,128)(2,1)S(1)}, bf16[32,4,768]{2,1,0:T(4,128)(2,1)S(1)}, u32[]{:S(2)}, u32[]{:S(2)}) %collective-permute-start.3) | collective-permute-done | bytes 196640 | tf_op jit(solution)/shard_map/return_owner/ppermute | solution.py:437
  132.3 0.0 copy-done
  132.3 0.0 copy-done.2
  132.3 0.0 copy-done.4
  132.3 0.0 copy-start.6
  132.3 0.7 copy-done.6
  133.0 0.0 collective-permute-done.2.refs_1_
  133.0 0.0 all-to-all-done.3
  133.0 4.3 %finish.1 = (f32[192,4,768]{2,1,0:T(4,128)}, bf16[2,1024,768]{2,1,0:T(8,128)(2,1)}) custom-call(s32[8,256]{1,0:T(8,128)S(1)} %get-tuple-element.39.table_ref, bf16[32,40,768]{2,1,0:T(8,128)(2,1)S(1)} %get-tuple-element.69.packed_ref, bf16[32,4,768]{2,1,0:T(4,128)(2,1)} %get-tuple-element.66.refs_0_, ...), custom_call_target="tpu_custom_call", output_to_operand_aliasing={{1}: (8, {})} | custom-call | tf_op jit(solution)/shard_map/finish/finish/pallas_call | solution.py:386
  (1 shorter events, 0.0 us)
Async XLA Ops:
  69.4 25.3 %all-to-all-start.2 = ((bf16[32,32,768]{2,1,0:T(8,128)(2,1)}), bf16[32,32,768]{2,1,0:T(8,128)(2,1)S(1)}, u32[]{:S(2)}, u32[]{:S(2)}) async-start(bf16[32,32,768]{2,1,0:T(8,128)(2,1)} %bitcast.5), calls=%async_computation.2 | async-start | bytes 3145728 | tf_op jit(solution)/shard_map/return_dp/all_to_all | solution.py:457
  74.8 16.3 %collective-permute-start = (bf16[32,4,768]{2,1,0:T(4,128)(2,1)S(1)}, bf16[32,4,768]{2,1,0:T(4,128)(2,1)S(1)}, u32[]{:S(2)}, u32[]{:S(2)}) collective-permute-start(bf16[32,4,768]{2,1,0:T(4,128)(2,1)S(1)} %get-tuple-element.67), channel_id=1, source_target_pairs={{0,3},{1,4},{2,5},{3,6},{4,7},{5,0},{6,1},{7,2},{8,11},{9,12},{10,... | collective-permute-start | bytes 589832 | tf_op jit(solution)/shard_map/return_owner_early/ppermute | solution.py:437
  75.5 15.7 %collective-permute-start.1 = (bf16[32,4,768]{2,1,0:T(4,128)(2,1)S(1)}, bf16[32,4,768]{2,1,0:T(4,128)(2,1)S(1)}, u32[]{:S(2)}, u32[]{:S(2)}) collective-permute-start(bf16[32,4,768]{2,1,0:T(4,128)(2,1)S(1)} %get-tuple-element.68), channel_id=1, source_target_pairs={{0,5},{1,6},{2,7},{3,0},{4,1},{5,2},{6,3},{7,4},{8,13},{9,14},{10,... | collective-permute-start | bytes 589832 | tf_op jit(solution)/shard_map/return_owner_early/ppermute | solution.py:437
  97.0 36.0 %all-to-all-start.3 = ((bf16[32,40,768]{2,1,0:T(8,128)(2,1)}), bf16[32,40,768]{2,1,0:T(8,128)(2,1)S(1)}, u32[]{:S(2)}, u32[]{:S(2)}) async-start(bf16[32,40,768]{2,1,0:T(8,128)(2,1)} %pack.1), calls=%async_computation.3 | async-start | bytes 3932160 | tf_op jit(solution)/shard_map/second_matrix/all_to_all | solution.py:465
  105.3 13.8 %collective-permute-start.6 = (bf16[32,4,768]{2,1,0:T(4,128)(2,1)S(1)}, bf16[32,4,768]{2,1,0:T(4,128)(2,1)S(1)}, u32[]{:S(2)}, u32[]{:S(2)}) collective-permute-start(bf16[32,4,768]{2,1,0:T(4,128)(2,1)S(1)} %get-tuple-element.61), channel_id=1, source_target_pairs={{0,7},{1,0},{2,1},{3,2},{4,3},{5,4},{6,5},{7,6},{8,15},{9,8},{10,9... | collective-permute-start | bytes 589832 | tf_op jit(solution)/shard_map/return_owner/ppermute | solution.py:437
  106.2 12.9 %collective-permute-start.5 = (bf16[32,4,768]{2,1,0:T(4,128)(2,1)S(1)}, bf16[32,4,768]{2,1,0:T(4,128)(2,1)S(1)}, u32[]{:S(2)}, u32[]{:S(2)}) collective-permute-start(bf16[32,4,768]{2,1,0:T(4,128)(2,1)S(1)} %get-tuple-element.62), channel_id=1, source_target_pairs={{0,1},{1,2},{2,3},{3,4},{4,5},{5,6},{6,7},{7,0},{8,9},{9,10},{10,1... | collective-permute-start | bytes 589832 | tf_op jit(solution)/shard_map/return_owner/ppermute | solution.py:437
  107.3 11.8 %collective-permute-start.4 = (bf16[32,4,768]{2,1,0:T(4,128)(2,1)S(1)}, bf16[32,4,768]{2,1,0:T(4,128)(2,1)S(1)}, u32[]{:S(2)}, u32[]{:S(2)}) collective-permute-start(bf16[32,4,768]{2,1,0:T(4,128)(2,1)S(1)} %get-tuple-element.63), channel_id=1, source_target_pairs={{0,6},{1,7},{2,0},{3,1},{4,2},{5,3},{6,4},{7,5},{8,14},{9,15},{10,... | collective-permute-start | bytes 589832 | tf_op jit(solution)/shard_map/return_owner/ppermute | solution.py:437
  110.8 21.5 %collective-permute-start.3 = (bf16[32,4,768]{2,1,0:T(4,128)(2,1)S(1)}, bf16[32,4,768]{2,1,0:T(4,128)(2,1)S(1)}, u32[]{:S(2)}, u32[]{:S(2)}) collective-permute-start(bf16[32,4,768]{2,1,0:T(4,128)(2,1)S(1)} %get-tuple-element.64), channel_id=1, source_target_pairs={{0,2},{1,3},{2,4},{3,5},{4,6},{5,7},{6,0},{7,1},{8,10},{9,11},{10,... | collective-permute-start | bytes 589832 | tf_op jit(solution)/shard_map/return_owner/ppermute | solution.py:437
  110.8 22.2 %collective-permute-start.2 = (bf16[32,4,768]{2,1,0:T(4,128)(2,1)S(1)}, bf16[32,4,768]{2,1,0:T(4,128)(2,1)}, u32[]{:S(2)}, u32[]{:S(2)}) collective-permute-start(bf16[32,4,768]{2,1,0:T(4,128)(2,1)S(1)} %get-tuple-element.65), channel_id=1, source_target_pairs={{0,4},{1,5},{2,6},{3,7},{4,0},{5,1},{6,2},{7,3},{8,12},{9,13},{10,... | collective-permute-start | bytes 589832 | tf_op jit(solution)/shard_map/return_owner/ppermute | solution.py:437
  119.1 13.2 %copy-start = (bf16[32,4,768]{2,1,0:T(4,128)(2,1)}, bf16[32,4,768]{2,1,0:T(4,128)(2,1)S(1)}, u32[]{:S(2)}) copy-start(bf16[32,4,768]{2,1,0:T(4,128)(2,1)S(1)} %collective-permute-done.6.refs_5_) | copy-start | bytes 589828
  119.1 13.2 %copy-start.2 = (bf16[32,4,768]{2,1,0:T(4,128)(2,1)}, bf16[32,4,768]{2,1,0:T(4,128)(2,1)S(1)}, u32[]{:S(2)}) copy-start(bf16[32,4,768]{2,1,0:T(4,128)(2,1)S(1)} %collective-permute-done.5.refs_4_) | copy-start | bytes 589828
  119.1 13.2 %copy-start.4 = (bf16[32,4,768]{2,1,0:T(4,128)(2,1)}, bf16[32,4,768]{2,1,0:T(4,128)(2,1)S(1)}, u32[]{:S(2)}) copy-start(bf16[32,4,768]{2,1,0:T(4,128)(2,1)S(1)} %collective-permute-done.4.refs_3_) | copy-start | bytes 589828
  132.3 0.7 copy-start.6
